TPU v7x, 32 devices: a whole 2x2x4 slice. The times are simulated.
32 devices in a mesh: groups: 2 (over y), adapter: 4 (over z), tensor: 4 (over x, core).
Axes of the slice: x: 2, y: 2, z: 4, core: 2. Of those that a mesh axis runs over, the one named last changes fastest.
Arguments:
- tokens: bfloat16 [6144, 8192], P(('groups', 'adapter'), 'tensor'), parts along dimension 0, may hold values from -6 to 6
- token_adapter_index: int32 [6144, 1], P(('groups', 'adapter')), parts along dimension 0, may hold values from 0 to 15; in each aligned block of 768 rows (0 to 767, 768 to 1535, ...) at most 96 rows name the same one
- adapter_page_index: int32 [16], replicated, may hold values from 0 to 15, each once
- value_base_weight: bfloat16 [8192, 1024], P('tensor'), may hold values from -0.0625 to 0.0625
- adapter_down_weight: bfloat16 [16, 64, 8192], P('adapter', None, 'tensor'), may hold values from -0.0625 to 0.0625
- adapter_up_weight: bfloat16 [16, 64, 1024], P('adapter'), may hold values from -0.75 to 0.75
Outputs:
- values: bfloat16 [6144, 1024], P(('groups', 'adapter'), 'tensor'), parts along dimension 0
There are 2 independent parts, one for each index of `groups`. A program takes and returns all parts, laid end to end along the dimension named above; an argument that names none is the same for every part. Nothing has to cross between parts.
Inputs may be any that keep to these rules, and one draw needn't show every extreme that they name: `token_adapter_index`: among the 768 tokens of one index of adapter (aligned blocks), no adapter is named by more than 96 tokens, a bound that some block reaches. Each page position belongs to exactly one adapter; adapter a's pages are row adapter_page_index[a] of adapter_down_weight and adapter_up_weight.
All inputs are finite; a program needn't handle non-finite values.
Results may differ from a plain program's by a relative error of at most 0.0042.
Values may be sent and summed in bfloat16 or wider, within the bound.
No kernel may reach another device: no remote copies, remote signals or barrier semaphores. Data moves between devices by JAX's collectives and lax.ppermute only.
A program may use at most 128 MiB of HBM per device.

v0:
```python
import jax
import jax.numpy as jnp
from jax import lax
from jax.sharding import PartitionSpec as P


def per_device(
    tokens,
    token_adapter_index,
    adapter_page_index,
    value_base_weight,
    adapter_down_weight,
    adapter_up_weight,
):
    tok_rows = tokens.shape[0]
    features = tokens.shape[1]
    holders = lax.axis_size("adapter")
    adapters = adapter_page_index.shape[0]
    resident_pages = adapter_down_weight.shape[0]
    capacity = 2 * tok_rows // adapters
    chosen = token_adapter_index[:, 0]
    onehot = (chosen[:, None] == jnp.arange(adapters, dtype=jnp.int32)[None, :]).astype(jnp.int32)
    position = jnp.sum(jnp.cumsum(onehot, axis=0) * onehot, axis=1) - 1
    page_number = jnp.sum(onehot * adapter_page_index[None, :], axis=1)
    slot = page_number * capacity + position
    outgoing = jnp.zeros((adapters * capacity, features), tokens.dtype).at[slot].set(tokens)
    outgoing = outgoing.reshape(holders, resident_pages * capacity, features)
    fetched_pages = lax.all_to_all(outgoing, "adapter", split_axis=0, concat_axis=0, tiled=True)
    fetched_pages = fetched_pages.reshape(holders, resident_pages, capacity, features)
    reduced_partial = jnp.einsum(
        "giod,iwd->giow", fetched_pages, adapter_down_weight, preferred_element_type=jnp.float32
    )
    reduced_partial = reduced_partial.astype(jnp.bfloat16)
    base_part = jnp.dot(tokens, value_base_weight, preferred_element_type=jnp.float32)
    delta_part = jnp.einsum(
        "stqk,tkh->stqh", reduced_partial, adapter_up_weight, preferred_element_type=jnp.float32
    )
    returned = lax.all_to_all(delta_part, "adapter", split_axis=0, concat_axis=0, tiled=True)
    returned = returned.reshape(adapters * capacity, delta_part.shape[3])
    summed = base_part + returned[slot]
    result = lax.psum_scatter(summed, "tensor", scatter_dimension=1, tiled=True)
    return result.astype(jnp.bfloat16)


def solution(mesh):
    placed = (
        P(("groups", "adapter"), "tensor"),
        P(("groups", "adapter"), None),
        P(),
        P("tensor", None),
        P("adapter", None, "tensor"),
        P("adapter", None, None),
    )
    return jax.shard_map(
        per_device,
        mesh=mesh,
        in_specs=placed,
        out_specs=P(("groups", "adapter"), "tensor"),
        check_vma=False,
    )
```

profile of v0, /device:TPU:0, one launch (start us, length us, event | category | flops | bytes accessed | tf_op | source)
XLA Modules:
  0.0 388.8 jit_solution(6182919417516705706)
XLA Ops:
  6.5 0.0 copy-start
  6.5 0.8 reduce
  7.3 1.7 reduce-window.6
  9.1 0.3 slice_reduce_fusion
  9.3 0.8 select_reduce_fusion
  10.1 11.6 %scatter_custom_fusion = bf16[1536,2048]{1,0:T(8,128)(2,1)} fusion(s32[768]{0:T(1024)S(1)} %fusion.18, bf16[768,2048]{1,0:T(8,128)(2,1)} %param.6, bf16[]{:T(256)} %constant.5.clone.1), kind=kCustom, calls=%fused_computation.4 | custom fusion | bytes 6291968 | tf_op jit(solution)/shard_map/scatter | solution.py:26
  21.7 0.0 copy-start.1
  21.7 146.6 %all_to_all.10 = bf16[4,384,2048]{2,1,0:T(8,128)(2,1)} all-to-all(bf16[4,384,2048]{2,1,0:T(8,128)(2,1)} %bitcast.40), channel_id=1, replica_groups=mesh['groups'=2,'adapter'=4,'tensor'=4] {'adapter'}, dimensions={0} | all-to-all | bytes 12582912 | tf_op jit(solution)/shard_map/all_to_all | solution.py:28
  168.4 0.0 copy-done
  168.4 0.0 copy-done.1
  168.4 8.7 %convolution_bitcast_fusion = f32[4,4,96,1024]{3,2,0,1:T(8,128)} fusion(bf16[4,4,96,2048]{3,2,1,0:T(8,128)(2,1)} %bitcast.41, bf16[4,64,2048]{2,1,0:T(8,128)(2,1)S(1)} %copy-done, bf16[4,64,1024]{2,1,0:T(8,128)(2,1)S(1)} %copy-done.1), kind=kOutput, calls=%fused_computation.6 | convolution fusion | flops 604078080 | bytes 14155776 | tf_op jit(solution)/shard_map/stqk,tkh->stqh/dot_general | solution.py:35
  177.0 6.5 %copy.13 = f32[4,4,96,1024]{3,2,1,0:T(8,128)} copy(f32[4,4,96,1024]{3,2,0,1:T(8,128)} %convolution_bitcast_fusion) | data formatting | bytes 12582912 | tf_op jit(solution)/shard_map/stqk,tkh->stqh/transpose | solution.py:35
  183.5 5.2 %all-to-all-start.1 = ((f32[4,4,96,1024]{3,2,1,0:T(8,128)}), f32[4,4,96,1024]{3,2,1,0:T(8,128)}, u32[]{:S(2)}, u32[]{:S(2)}) async-start(f32[4,4,96,1024]{3,2,1,0:T(8,128)} %copy.13), calls=%async_computation.1 | async-start | bytes 12582912 | tf_op jit(solution)/shard_map/all_to_all | solution.py:38
  188.8 0.2 reduce-scatter.2.cloned.1.call-start
  189.0 137.6 %all-to-all-done.1 = f32[4,4,96,1024]{3,2,1,0:T(8,128)} async-done(((f32[4,4,96,1024]{3,2,1,0:T(8,128)}), f32[4,4,96,1024]{3,2,1,0:T(8,128)}, u32[]{:S(2)}, u32[]{:S(2)}) %all-to-all-start.1) | async-done | bytes 6291488 | tf_op jit(solution)/shard_map/all_to_all | solution.py:38
  326.6 7.5 %gather_fusion = f32[768,1024]{1,0:T(8,128)} fusion(f32[1536,1024]{1,0:T(8,128)} %bitcast.9, s32[1024]{0:T(1024)S(1)} %pad_clamp_fusion), kind=kCustom, calls=%fused_computation | custom fusion | bytes 6294528 | tf_op jit(solution)/shard_map/gather | solution.py:40
  334.2 9.2 %convolution_add_fusion = f32[768,1024]{1,0:T(8,128)} fusion(f32[768,1024]{1,0:T(8,128)} %gather_fusion, bf16[768,2048]{1,0:T(8,128)(2,1)} %param.6, bf16[2048,1024]{1,0:T(8,128)(2,1)} %param.9), kind=kOutput, calls=%fused_computation.7 | convolution fusion | flops 3222011904 | bytes 13631488 | tf_op jit(solution)/shard_map/dot_general | solution.py:34
  343.4 0.0 reduce-scatter.2.cloned.1.call-update
  343.4 36.7 %reduce-scatter.2.cloned.1.call-done = f32[768,256]{1,0:T(8,128)} async-done(((f32[768,1024]{1,0:T(8,128)}), f32[768,256]{1,0:T(8,128)}) %reduce-scatter.2.cloned.1.call-update) | async-done | bytes 786448 | tf_op jit(solution)/shard_map/reduce_scatter | solution.py:41
  380.1 1.9 convert_element_type.17
  (5 shorter events, 0.1 us)
Async XLA Ops:
  6.5 161.8 %copy-start = (bf16[4,64,2048]{2,1,0:T(8,128)(2,1)S(1)}, bf16[4,64,2048]{2,1,0:T(8,128)(2,1)}, u32[]{:S(2)}) copy-start(bf16[4,64,2048]{2,1,0:T(8,128)(2,1)} %param.10) | copy-start | bytes 3145732
  21.7 146.6 %copy-start.1 = (bf16[4,64,1024]{2,1,0:T(8,128)(2,1)S(1)}, bf16[4,64,1024]{2,1,0:T(8,128)(2,1)}, u32[]{:S(2)}) copy-start(bf16[4,64,1024]{2,1,0:T(8,128)(2,1)} %param.11) | copy-start | bytes 1572868
  183.5 143.1 %all-to-all-start.1 = ((f32[4,4,96,1024]{3,2,1,0:T(8,128)}), f32[4,4,96,1024]{3,2,1,0:T(8,128)}, u32[]{:S(2)}, u32[]{:S(2)}) async-start(f32[4,4,96,1024]{3,2,1,0:T(8,128)} %copy.13), calls=%async_computation.1 | async-start | bytes 12582912 | tf_op jit(solution)/shard_map/all_to_all | solution.py:38
  188.8 191.3 %reduce-scatter.2.cloned.1.call-start = ((), (), s32[]{:S(2)}) async-start(), calls=%async_computation.3 | async-start | bytes 3932160 | tf_op jit(solution)/shard_map/reduce_scatter | solution.py:41
Sparse Core Ops, SparseCore 0:
  343.5 36.5 reduce-scatter.1
where the time goes:
time: 389 us
  waiting for transfers between devices  174 us (45%)
  blocking collectives  147 us (38%)
  local copies, waits for them, and re-layouts  25.9 us (7%)
  matrix products  17.8 us (5%)
  between operations  13.5 us (3%)
  starting transfers between devices  5.46 us (1%)
  other arithmetic  5.23 us (1%)
    all_to_all x1, blocking collectives, per_device(): lax.all_to_all(outgoing, 'adapter', split_axis=0, concat_axis=0, tiled=True)  147 us
    all_to_all x1, waiting for transfers between devices, per_device(): lax.all_to_all(delta_part, 'adapter', split_axis=0, concat_axis=0, tiled=...  138 us
    reduce_scatter x1, waiting for transfers between devices, per_device(): result = lax.psum_scatter(summed, 'tensor', scatter_dimension=1, tiled=True)  36.7 us
    scatter x1, local copies, waits for them, and re-layouts, per_device(): jnp.zeros((adapters * capacity, features), tokens.dtype).at[slot]  11.6 us
    dot_general x1, matrix products, per_device(): jnp.dot(tokens, value_base_weight, preferred_element_type=jnp.float32)  9.17 us
    dot_general x1, matrix products, per_device(): jnp.einsum('stqk,tkh->stqh', reduced_partial, adapter_up_weight, preferre...  8.66 us
  transfers between devices with their start and end apart: 2, of which 2 were waited for; matrix products, arithmetic and copies ran while one was open for 0% of the time, Pallas kernels for 0%

commit v1 on v0

v1 whole, which is shorter than its diff:
```python
import jax
import jax.numpy as jnp
from jax import lax
from jax.sharding import PartitionSpec as P

F32 = jnp.float32
BF16 = jnp.bfloat16


def swap(x, axis, size, bit):
    return lax.ppermute(x, axis, [(i, i ^ bit) for i in range(size)])


def spread_over_holders(piece, axis, size):
    me = lax.axis_index(axis)
    if size == 4:
        near = swap(piece, axis, size, 1)
        far = swap(piece, axis, size, 2)
        middle = lax.ppermute(piece, axis, [(1, 2), (2, 1)])
        ends = lax.ppermute(far, axis, [(1, 0), (2, 3)])
        inner = (me == 1) | (me == 2)
        last = jnp.where(inner, middle, ends)
        return [(near, me ^ 1), (far, me ^ 2), (last, 3 - me)]
    found = []
    for step in range(1, size):
        piece = lax.ppermute(piece, axis, [(i, (i - 1) % size) for i in range(size)])
        found.append((piece, (me + step) % size))
    return found


def share_base(tokens, weight, axis, size):
    me = lax.axis_index(axis)
    block = weight.shape[1] // size
    if size & (size - 1):
        whole = jnp.dot(tokens, weight, preferred_element_type=F32)
        return lax.psum_scatter(whole, axis, scatter_dimension=1, tiled=True)

    def half(bit):
        columns = [lax.dynamic_slice_in_dim(weight, (2 * m + bit) * block, block, axis=1) for m in range(size // 2)]
        return jnp.dot(tokens, jnp.concatenate(columns, axis=1), preferred_element_type=F32)

    mine = me & 1
    held = half(mine) + swap(half(1 - mine), axis, size, 1)
    bit = 2
    while bit < size:
        mine = (me // bit) & 1
        count = held.shape[1] // block

        def pick(which):
            return jnp.concatenate(
                [lax.dynamic_slice_in_dim(held, (2 * m + which) * block, block, axis=1) for m in range(count // 2)],
                axis=1,
            )

        held = pick(mine) + swap(pick(1 - mine), axis, size, bit)
        bit *= 2
    return held


def make(sizes):
    groups, holders, tensor = sizes["groups"], sizes["adapter"], sizes["tensor"]

    def per_device(tokens, token_adapter_index, adapter_page_index, base_weight, down, up):
        rows, features = tokens.shape
        resident, rank, width = up.shape
        adapters = adapter_page_index.shape[0]
        block = width // tensor
        shared = groups if resident % groups == 0 else 1
        part = resident // shared
        group, holder, share = lax.axis_index("groups"), lax.axis_index("adapter"), lax.axis_index("tensor")

        chosen = token_adapter_index[:, 0]
        onehot = chosen[None, :] == jnp.arange(adapters, dtype=jnp.int32)[:, None]
        page = jnp.sum(jnp.where(onehot, adapter_page_index[:, None], 0), axis=0)

        up_mine = lax.dynamic_slice_in_dim(up.reshape(resident * rank, width), share * block, block, axis=1)
        own = jnp.concatenate([down.reshape(resident * rank, features), up_mine], axis=1)
        pieces = [(own, holder * resident)]
        mine = group if shared > 1 else 0
        sent = lax.dynamic_slice_in_dim(own, mine * part * rank, part * rank, axis=0)
        for piece, source in spread_over_holders(sent, "adapter", holders):
            pieces.append((piece, source * resident + mine * part))
            for step in range(1, shared):
                other = lax.ppermute(piece, "groups", [(i, (i + step) % shared) for i in range(shared)])
                pieces.append((other, source * resident + (group - step) % shared * part))

        base = share_base(tokens, base_weight, "tensor", tensor)

        shrink = jnp.zeros((rank, rows), F32)
        for piece, first in pieces:
            product = lax.dot_general(piece[:, :features], tokens, (((1,), (1,)), ((), ())), preferred_element_type=F32)
            for k in range(piece.shape[0] // rank):
                shrink = shrink + jnp.where(page[None, :] == first + k, product[k * rank : (k + 1) * rank], 0.0)
        shrink = shrink.astype(BF16)
        total = shrink.astype(F32)
        for step in range(1, tensor):
            other = lax.ppermute(shrink, "tensor", [(i, (i + step) % tensor) for i in range(tensor)])
            total = total + other.astype(F32)
        total = total.astype(BF16)

        ups = jnp.concatenate([piece[:, features:] for piece, _ in pieces], axis=0)
        spread = jnp.concatenate(
            [
                jnp.where(page[None, :] == first + k, total, 0)
                for piece, first in pieces
                for k in range(piece.shape[0] // rank)
            ],
            axis=0,
        )
        delta = lax.dot_general(spread, ups, (((0,), (0,)), ((), ())), preferred_element_type=F32)
        return (base + delta).astype(BF16)

    return per_device


def solution(mesh):
    placed = (
        P(("groups", "adapter"), "tensor"),
        P(("groups", "adapter"), None),
        P(),
        P("tensor", None),
        P("adapter", None, "tensor"),
        P("adapter", None, None),
    )
    return jax.shard_map(
        make(dict(mesh.shape)),
        mesh=mesh,
        in_specs=placed,
        out_specs=P(("groups", "adapter"), "tensor"),
        check_vma=False,
    )
```

time: 389 us -> 97 us (0.25)
  the two profiles are of different devices: /device:TPU:0 before, /device:TPU:17 now
where the time goes in v1:
time: 97 us; the launch traced here: 96.5 us
  waiting for transfers between devices  44.1 us (45%)
  starting transfers between devices  20.3 us (21%)
  matrix products  19.1 us (20%)
  local copies, waits for them, and re-layouts  8.67 us (9%)
  other arithmetic  3.95 us (4%)
    ppermute x3, waiting for transfers between devices, per_device(): lax.ppermute(piece, 'groups', [(i, (i + step) % shared) for i in range(sh...  15.4 us
    ppermute x3, waiting for transfers between devices, per_device(): lax.ppermute(shrink, 'tensor', [(i, (i + step) % tensor) for i in range(t...  14 us
    dot_general x7, matrix products, per_device(): lax.dot_general(piece[:, :features], tokens, (((1,), (1,)), ((), ())), pr...  12.3 us
    ppermute x4, waiting for transfers between devices, swap(): return lax.ppermute(x, axis, [(i, i ^ bit) for i in range(size)])  9.36 us
    ppermute x1, starting transfers between devices, spread_over_holders(): ends = lax.ppermute(far, axis, [(1, 0), (2, 3)])  6.94 us
    dot_general x2, matrix products, half(): jnp.dot(tokens, jnp.concatenate(columns, axis=1), preferred_element_type=...  6.22 us
    ppermute x1, starting transfers between devices, spread_over_holders(): middle = lax.ppermute(piece, axis, [(1, 2), (2, 1)])  4.37 us
    dynamic_slice x1, local copies, waits for them, and re-layouts, half(): lax.dynamic_slice_in_dim(weight, (2 * m + bit) * block, block, axis=1)  3.86 us
  transfers between devices with their start and end apart: 12, of which 7 were waited for; matrix products, arithmetic and copies ran while one was open for 27% of the time, Pallas kernels for 0%

profile of v1, /device:TPU:17, one launch (start us, length us, event | category | flops | bytes accessed | tf_op | source)
XLA Modules:
  0.0 96.5 jit_solution(2398714678343261894)
XLA Ops:
  0.0 1.7 %constant_dynamic-update-slice_fusion = (bf16[1024,256]{1,0:T(8,128)(2,1)}, bf16[256,256]{1,0:T(8,128)(2,1)S(1)}) fusion(bf16[256,1024]{1,0:T(8,128)(2,1)} %bitcast.20, s32[]{:T(128)S(6)} %select_n.161), kind=kLoop, calls=%fused_computation.84 | loop fusion | bytes 393220
  1.7 1.9 %fusion.13 = bf16[128,2304]{1,0:T(8,128)(2,1)} fusion(s32[]{:T(128)S(6)} %select_n.162, bf16[256,2048]{1,0:T(8,128)(2,1)} %bitcast.18, bf16[256,256]{1,0:T(8,128)(2,1)S(1)} %get-tuple-element.6), kind=kLoop, calls=%fused_computation.13 | loop fusion | flops 1179648 | bytes 1769476 | tf_op jit(solution)/shard_map/concatenate | solution.py:77
  3.6 0.0 collective-permute-start.4
  3.6 4.4 %collective-permute-start.6 = (bf16[128,2304]{1,0:T(8,128)(2,1)}, bf16[128,2304]{1,0:T(8,128)(2,1)}, u32[]{:S(2)}, u32[]{:S(2)}) collective-permute-start(bf16[128,2304]{1,0:T(8,128)(2,1)} %fusion.13), channel_id=1, source_target_pairs={{4,8},{8,4},{5,9},{9,5},{6,10},{10,6},{7,11},{11,7},{20,24},{24,20... | collective-permute-start | bytes 1769480 | tf_op jit(solution)/shard_map/ppermute | solution.py:19
  8.0 0.1 collective-permute-start.2
  8.1 3.9 %constant_dynamic-slice_fusion.5 = (bf16[2048,256]{1,0:T(8,128)(2,1)}, bf16[2048,256]{1,0:T(8,128)(2,1)}, bf16[2048,256]{1,0:T(8,128)(2,1)S(1)}, bf16[2048,256]{1,0:T(8,128)(2,1)S(1)}) fusion(bf16[2048,1024]{1,0:T(8,128)(2,1)} %param.9, s32[]{:T(128)S(6)} %select_n.149, s32[]{:T(128)S(6)} %select_n.150, s32[]{:T(128)S(6)} %select_n.152, s32[]{:T(128)S(6)} %select_n.151), kind=kLoop, calls=%fused_computation.90 | loop fusion | bytes 8388624 | tf_op jit(solution)/shard_map/dynamic_slice | solution.py:39
  12.0 3.0 %fusion.8 = f32[768,512]{0,1:T(8,128)} fusion(bf16[768,2048]{1,0:T(8,128)(2,1)S(1)} %copy-done, bf16[2048,256]{1,0:T(8,128)(2,1)S(1)} %get-tuple-element.11, bf16[2048,256]{1,0:T(8,128)(2,1)S(1)} %get-tuple-element.12), kind=kOutput, calls=%fused_computation.9 | convolution fusion | flops 1614807040 | bytes 6815744 | tf_op jit(solution)/shard_map/dot_general | solution.py:40
  14.9 1.2 %collective-permute-start = (f32[768,512]{0,1:T(8,128)}, f32[768,512]{0,1:T(8,128)}, u32[]{:S(2)}, u32[]{:S(2)}) collective-permute-start(f32[768,512]{0,1:T(8,128)} %fusion.8), channel_id=1, source_target_pairs={{0,1},{1,0},{2,3},{3,2},{4,5},{5,4},{6,7},{7,6},{8,9},{9,8},{10,11... | collective-permute-start | bytes 4718600 | tf_op jit(solution)/shard_map/ppermute | solution.py:11
  16.2 0.0 copy-start.6
  16.2 3.2 %fusion.44 = f32[256,768]{1,0:T(8,128)} fusion(bf16[256,2048]{1,0:T(8,128)(2,1)} %bitcast.19, bf16[768,2048]{1,0:T(8,128)(2,1)S(1)} %copy-done), kind=kOutput, calls=%fused_computation.109 | convolution fusion | flops 805306368 | bytes 4980736 | tf_op jit(solution)/shard_map/dot_general | solution.py:91
  19.4 0.1 select_reduce_fusion
  19.6 9.4 %collective-permute-done.4 = bf16[128,2304]{1,0:T(8,128)(2,1)} collective-permute-done((bf16[128,2304]{1,0:T(8,128)(2,1)}, bf16[128,2304]{1,0:T(8,128)(2,1)}, u32[]{:S(2)}, u32[]{:S(2)}) %collective-permute-start.4) | collective-permute-done | bytes 589856 | tf_op jit(solution)/shard_map/ppermute | solution.py:11
  28.9 6.9 %collective-permute-start.7 = (bf16[128,2304]{1,0:T(8,128)(2,1)}, bf16[128,2304]{1,0:T(8,128)(2,1)S(1)}, u32[]{:S(2)}, u32[]{:S(2)}) collective-permute-start(bf16[128,2304]{1,0:T(8,128)(2,1)} %collective-permute-done.4), channel_id=1, source_target_pairs={{4,0},{8,12},{5,1},{9,13},{6,2},{10,14},{7,3},{11,15},{20,16},{24,... | collective-permute-start | bytes 1769480 | tf_op jit(solution)/shard_map/ppermute | solution.py:20
  35.9 1.3 %collective-permute-start.5 = (bf16[128,2304]{1,0:T(8,128)(2,1)}, bf16[128,2304]{1,0:T(8,128)(2,1)S(1)}, u32[]{:S(2)}, u32[]{:S(2)}) collective-permute-start(bf16[128,2304]{1,0:T(8,128)(2,1)} %collective-permute-done.4), channel_id=1, source_target_pairs={{0,16},{16,0},{1,17},{17,1},{2,18},{18,2},{3,19},{19,3},{4,20},{20... | collective-permute-start | bytes 1769480 | tf_op jit(solution)/shard_map/ppermute | solution.py:84
  37.2 2.2 %fusion.20 = f32[128,768]{1,0:T(8,128)S(1)} fusion(bf16[768,2048]{1,0:T(8,128)(2,1)S(1)} %copy-done, bf16[128,2304]{1,0:T(8,128)(2,1)} %collective-permute-done.4), kind=kOutput, calls=%fused_computation.21 | convolution fusion | flops 402653184 | bytes 4063232 | tf_op jit(solution)/shard_map/dot_general | solution.py:91
  39.5 0.0 collective-permute-done.2
  39.5 0.3 collective-permute-start.3
  39.8 0.9 slice_dynamic-update-slice_fusion.5
  40.6 2.2 %fusion.24 = f32[128,768]{1,0:T(8,128)S(1)} fusion(bf16[768,2048]{1,0:T(8,128)(2,1)S(1)} %copy-done, bf16[128,2304]{1,0:T(8,128)(2,1)} %collective-permute-done.2), kind=kOutput, calls=%fused_computation.25 | convolution fusion | flops 402653184 | bytes 4063232 | tf_op jit(solution)/shard_map/dot_general | solution.py:91
  42.9 2.6 %collective-permute-done.6 = bf16[128,2304]{1,0:T(8,128)(2,1)} collective-permute-done((bf16[128,2304]{1,0:T(8,128)(2,1)}, bf16[128,2304]{1,0:T(8,128)(2,1)}, u32[]{:S(2)}, u32[]{:S(2)}) %collective-permute-start.6) | collective-permute-done | bytes 589856 | tf_op jit(solution)/shard_map/ppermute | solution.py:19
  45.4 2.8 %collective-permute-done.7 = bf16[128,2304]{1,0:T(8,128)(2,1)S(1)} collective-permute-done((bf16[128,2304]{1,0:T(8,128)(2,1)}, bf16[128,2304]{1,0:T(8,128)(2,1)S(1)}, u32[]{:S(2)}, u32[]{:S(2)}) %collective-permute-start.7) | collective-permute-done | bytes 589856 | tf_op jit(solution)/shard_map/ppermute | solution.py:20
  48.3 1.1 %broadcast_select_fusion = bf16[128,2304]{1,0:T(8,128)(2,1)S(1)} fusion(bf16[128,2304]{1,0:T(8,128)(2,1)} %collective-permute-done.6, bf16[128,2304]{1,0:T(8,128)(2,1)S(1)} %collective-permute-done.7, pred[]{:T(512)S(6)} %or.3), kind=kLoop, calls=%fused_computation.14 | loop fusion | flops 294912 | bytes 1769473 | tf_op jit(solution)/shard_map/jit(_where)/select_n | solution.py:22
  49.4 1.3 %collective-permute-start.8 = (bf16[128,2304]{1,0:T(8,128)(2,1)S(1)}, bf16[128,2304]{1,0:T(8,128)(2,1)S(1)}, u32[]{:S(2)}, u32[]{:S(2)}) collective-permute-start(bf16[128,2304]{1,0:T(8,128)(2,1)S(1)} %broadcast_select_fusion), channel_id=1, source_target_pairs={{0,16},{16,0},{1,17},{17,1},{2,18},{18,2},{3,19},{19,3},{4,20},{20... | collective-permute-start | bytes 1769480 | tf_op jit(solution)/shard_map/ppermute | solution.py:84
  50.7 12.1 %collective-permute-done.3 = bf16[128,2304]{1,0:T(8,128)(2,1)S(1)} collective-permute-done((bf16[128,2304]{1,0:T(8,128)(2,1)}, bf16[128,2304]{1,0:T(8,128)(2,1)S(1)}, u32[]{:S(2)}, u32[]{:S(2)}) %collective-permute-start.3) | collective-permute-done | bytes 589856 | tf_op jit(solution)/shard_map/ppermute | solution.py:84
  62.8 0.8 slice_dynamic-update-slice_fusion.3
  63.6 0.0 collective-permute-done.5
  63.7 1.2 %fusion.16 = f32[128,768]{1,0:T(8,128)S(1)} fusion(bf16[768,2048]{1,0:T(8,128)(2,1)S(1)} %copy-done, bf16[128,2304]{1,0:T(8,128)(2,1)S(1)} %broadcast_select_fusion), kind=kOutput, calls=%fused_computation.17 | convolution fusion | flops 402653184 | bytes 4063232 | tf_op jit(solution)/shard_map/dot_general | solution.py:91
  64.8 1.2 %fusion.18 = f32[128,768]{1,0:T(8,128)S(1)} fusion(bf16[768,2048]{1,0:T(8,128)(2,1)S(1)} %copy-done, bf16[128,2304]{1,0:T(8,128)(2,1)S(1)} %collective-permute-done.5), kind=kOutput, calls=%fused_computation.19 | convolution fusion | flops 402653184 | bytes 4063232 | tf_op jit(solution)/shard_map/dot_general | solution.py:91
  66.0 1.2 %fusion.22 = f32[128,768]{1,0:T(8,128)S(1)} fusion(bf16[768,2048]{1,0:T(8,128)(2,1)S(1)} %copy-done, bf16[128,2304]{1,0:T(8,128)(2,1)S(1)} %collective-permute-done.3), kind=kOutput, calls=%fused_computation.23 | convolution fusion | flops 402653184 | bytes 4063232 | tf_op jit(solution)/shard_map/dot_general | solution.py:91
  67.2 0.0 collective-permute-done
  67.2 0.0 copy-done.1
  67.2 0.3 copy-done.2
  67.6 3.2 %bitcast_add_fusion = f32[768,512]{0,1:T(8,128)S(1)} fusion(f32[768,512]{0,1:T(8,128)} %collective-permute-done, bf16[768,2048]{1,0:T(8,128)(2,1)S(1)} %copy-done, bf16[2048,256]{1,0:T(8,128)(2,1)S(1)} %copy-done.2, bf16[2048,256]{1,0:T(8,128)(2,1)S(1)} %copy-done.1), kind=kOutput, calls=%fused_computation.8 | convolution fusion | flops 1615200256 | bytes 8388608 | tf_op jit(solution)/shard_map/dot_general | solution.py:40
  70.8 0.1 constant_dynamic-slice_fusion.1
  70.9 1.3 %collective-permute-start.1 = (f32[768,256]{0,1:T(8,128)S(1)}, f32[768,256]{0,1:T(8,128)S(1)}, u32[]{:S(2)}, u32[]{:S(2)}) collective-permute-start(f32[768,256]{0,1:T(8,128)S(1)} %constant_dynamic-slice_fusion.1), channel_id=1, source_target_pairs={{0,2},{1,3},{2,0},{3,1},{4,6},{5,7},{6,4},{7,5},{8,10},{9,11},{10,... | collective-permute-start | bytes 2359304 | tf_op jit(solution)/shard_map/ppermute | solution.py:11
  72.2 3.3 %collective-permute-done.8 = bf16[128,2304]{1,0:T(8,128)(2,1)S(1)} collective-permute-done((bf16[128,2304]{1,0:T(8,128)(2,1)S(1)}, bf16[128,2304]{1,0:T(8,128)(2,1)S(1)}, u32[]{:S(2)}, u32[]{:S(2)}) %collective-permute-start.8) | collective-permute-done | bytes 589856 | tf_op jit(solution)/shard_map/ppermute | solution.py:84
  75.4 1.2 %fusion.14 = f32[128,768]{1,0:T(8,128)S(1)} fusion(bf16[768,2048]{1,0:T(8,128)(2,1)S(1)} %copy-done, bf16[128,2304]{1,0:T(8,128)(2,1)S(1)} %collective-permute-done.8), kind=kOutput, calls=%fused_computation.15 | convolution fusion | flops 402653184 | bytes 4063232 | tf_op jit(solution)/shard_map/dot_general | solution.py:91
  76.6 0.4 fusion.27
  77.0 1.3 %collective-permute-start.10 = (bf16[64,768]{1,0:T(8,128)(2,1)S(1)}, bf16[64,768]{1,0:T(8,128)(2,1)S(1)}, u32[]{:S(2)}, u32[]{:S(2)}) collective-permute-start(bf16[64,768]{1,0:T(8,128)(2,1)S(1)} %fusion.27), channel_id=1, source_target_pairs={{0,2},{1,3},{2,0},{3,1},{4,6},{5,7},{6,4},{7,5},{8,10},{9,11},{10,... | collective-permute-start | bytes 294920 | tf_op jit(solution)/shard_map/ppermute | solution.py:97
  78.3 2.0 %collective-permute-start.11 = (bf16[64,768]{1,0:T(8,128)(2,1)S(1)}, bf16[64,768]{1,0:T(8,128)(2,1)S(1)}, u32[]{:S(2)}, u32[]{:S(2)}) collective-permute-start(bf16[64,768]{1,0:T(8,128)(2,1)S(1)} %fusion.27), channel_id=1, source_target_pairs={{0,3},{1,0},{2,1},{3,2},{4,7},{5,4},{6,5},{7,6},{8,11},{9,8},{10,9... | collective-permute-start | bytes 294920 | tf_op jit(solution)/shard_map/ppermute | solution.py:97
  80.3 0.1 collective-permute-start.9
  80.5 8.5 %collective-permute-done.10 = bf16[64,768]{1,0:T(8,128)(2,1)S(1)} collective-permute-done((bf16[64,768]{1,0:T(8,128)(2,1)S(1)}, bf16[64,768]{1,0:T(8,128)(2,1)S(1)}, u32[]{:S(2)}, u32[]{:S(2)}) %collective-permute-start.10) | collective-permute-done | bytes 98336 | tf_op jit(solution)/shard_map/ppermute | solution.py:97
  89.0 5.5 %collective-permute-done.11 = bf16[64,768]{1,0:T(8,128)(2,1)S(1)} collective-permute-done((bf16[64,768]{1,0:T(8,128)(2,1)S(1)}, bf16[64,768]{1,0:T(8,128)(2,1)S(1)}, u32[]{:S(2)}, u32[]{:S(2)}) %collective-permute-start.11) | collective-permute-done | bytes 98336 | tf_op jit(solution)/shard_map/ppermute | solution.py:97
  94.4 0.0 collective-permute-done.9
  94.4 0.1 select_dynamic-update-slice_fusion.15
  95.0 0.0 collective-permute-done.1
  95.0 0.6 add_convert_fusion
  95.6 0.9 copy.10
  (32 shorter events, 0.4 us)
Async XLA Ops:
  0.0 12.0 %copy-start = (bf16[768,2048]{1,0:T(8,128)(2,1)S(1)}, bf16[768,2048]{1,0:T(8,128)(2,1)}, u32[]{:S(2)}) copy-start(bf16[768,2048]{1,0:T(8,128)(2,1)} %param.6) | copy-start | bytes 9437188
  3.6 25.3 %collective-permute-start.4 = (bf16[128,2304]{1,0:T(8,128)(2,1)}, bf16[128,2304]{1,0:T(8,128)(2,1)}, u32[]{:S(2)}, u32[]{:S(2)}) collective-permute-start(bf16[128,2304]{1,0:T(8,128)(2,1)} %fusion.13), channel_id=1, source_target_pairs={{0,8},{4,12},{8,0},{12,4},{1,9},{5,13},{9,1},{13,5},{2,10},{6,14},... | collective-permute-start | bytes 1769480 | tf_op jit(solution)/shard_map/ppermute | solution.py:11
  3.6 41.8 %collective-permute-start.6 = (bf16[128,2304]{1,0:T(8,128)(2,1)}, bf16[128,2304]{1,0:T(8,128)(2,1)}, u32[]{:S(2)}, u32[]{:S(2)}) collective-permute-start(bf16[128,2304]{1,0:T(8,128)(2,1)} %fusion.13), channel_id=1, source_target_pairs={{4,8},{8,4},{5,9},{9,5},{6,10},{10,6},{7,11},{11,7},{20,24},{24,20... | collective-permute-start | bytes 1769480 | tf_op jit(solution)/shard_map/ppermute | solution.py:19
  8.0 31.4 %collective-permute-start.2 = (bf16[128,2304]{1,0:T(8,128)(2,1)}, bf16[128,2304]{1,0:T(8,128)(2,1)}, u32[]{:S(2)}, u32[]{:S(2)}) collective-permute-start(bf16[128,2304]{1,0:T(8,128)(2,1)} %fusion.13), channel_id=1, source_target_pairs={{0,4},{4,0},{8,12},{12,8},{1,5},{5,1},{9,13},{13,9},{2,6},{6,2},{1... | collective-permute-start | bytes 1769480 | tf_op jit(solution)/shard_map/ppermute | solution.py:11
  12.0 4.2 %copy-start.5 = (s32[768,1]{0,1:T(1,128)S(1)}, s32[768,1]{0,1:T(1,128)}, u32[]{:S(2)}) copy-start(s32[768,1]{0,1:T(1,128)} %param.7) | copy-start | bytes 9220
  14.9 52.3 %collective-permute-start = (f32[768,512]{0,1:T(8,128)}, f32[768,512]{0,1:T(8,128)}, u32[]{:S(2)}, u32[]{:S(2)}) collective-permute-start(f32[768,512]{0,1:T(8,128)} %fusion.8), channel_id=1, source_target_pairs={{0,1},{1,0},{2,3},{3,2},{4,5},{5,4},{6,7},{7,6},{8,9},{9,8},{10,11... | collective-permute-start | bytes 4718600 | tf_op jit(solution)/shard_map/ppermute | solution.py:11
  16.2 3.2 %copy-start.6 = (s32[16]{0:T(128)S(1)}, s32[16]{0:T(128)}, u32[]{:S(2)}) copy-start(s32[16]{0:T(128)} %param.8) | copy-start | bytes 196
  19.6 20.2 %copy-start.3 = (bf16[1024,256]{1,0:T(8,128)(2,1)S(1)}, bf16[1024,256]{1,0:T(8,128)(2,1)}, u32[]{:S(2)}) copy-start(bf16[1024,256]{1,0:T(8,128)(2,1)} %get-tuple-element.5) | copy-start | bytes 1572868
  28.9 19.3 %collective-permute-start.7 = (bf16[128,2304]{1,0:T(8,128)(2,1)}, bf16[128,2304]{1,0:T(8,128)(2,1)S(1)}, u32[]{:S(2)}, u32[]{:S(2)}) collective-permute-start(bf16[128,2304]{1,0:T(8,128)(2,1)} %collective-permute-done.4), channel_id=1, source_target_pairs={{4,0},{8,12},{5,1},{9,13},{6,2},{10,14},{7,3},{11,15},{20,16},{24,... | collective-permute-start | bytes 1769480 | tf_op jit(solution)/shard_map/ppermute | solution.py:20
  35.9 27.7 %collective-permute-start.5 = (bf16[128,2304]{1,0:T(8,128)(2,1)}, bf16[128,2304]{1,0:T(8,128)(2,1)S(1)}, u32[]{:S(2)}, u32[]{:S(2)}) collective-permute-start(bf16[128,2304]{1,0:T(8,128)(2,1)} %collective-permute-done.4), channel_id=1, source_target_pairs={{0,16},{16,0},{1,17},{17,1},{2,18},{18,2},{3,19},{19,3},{4,20},{20... | collective-permute-start | bytes 1769480 | tf_op jit(solution)/shard_map/ppermute | solution.py:84
  39.5 23.3 %collective-permute-start.3 = (bf16[128,2304]{1,0:T(8,128)(2,1)}, bf16[128,2304]{1,0:T(8,128)(2,1)S(1)}, u32[]{:S(2)}, u32[]{:S(2)}) collective-permute-start(bf16[128,2304]{1,0:T(8,128)(2,1)} %collective-permute-done.2), channel_id=1, source_target_pairs={{0,16},{16,0},{1,17},{17,1},{2,18},{18,2},{3,19},{19,3},{4,20},{20... | collective-permute-start | bytes 1769480 | tf_op jit(solution)/shard_map/ppermute | solution.py:84
  49.4 26.0 %collective-permute-start.8 = (bf16[128,2304]{1,0:T(8,128)(2,1)S(1)}, bf16[128,2304]{1,0:T(8,128)(2,1)S(1)}, u32[]{:S(2)}, u32[]{:S(2)}) collective-permute-start(bf16[128,2304]{1,0:T(8,128)(2,1)S(1)} %broadcast_select_fusion), channel_id=1, source_target_pairs={{0,16},{16,0},{1,17},{17,1},{2,18},{18,2},{3,19},{19,3},{4,20},{20... | collective-permute-start | bytes 1769480 | tf_op jit(solution)/shard_map/ppermute | solution.py:84
  66.0 1.2 %copy-start.1 = (bf16[2048,256]{1,0:T(8,128)(2,1)S(1)}, bf16[2048,256]{1,0:T(8,128)(2,1)}, u32[]{:S(2)}) copy-start(bf16[2048,256]{1,0:T(8,128)(2,1)} %get-tuple-element.9) | copy-start | bytes 3145732
  66.0 1.5 %copy-start.2 = (bf16[2048,256]{1,0:T(8,128)(2,1)S(1)}, bf16[2048,256]{1,0:T(8,128)(2,1)}, u32[]{:S(2)}) copy-start(bf16[2048,256]{1,0:T(8,128)(2,1)} %get-tuple-element.10) | copy-start | bytes 3145732
  70.9 5.7 %copy-start.4 = (f32[256,768]{1,0:T(8,128)S(1)}, f32[256,768]{1,0:T(8,128)}, u32[]{:S(2)}) copy-start(f32[256,768]{1,0:T(8,128)} %fusion.44) | copy-start | bytes 2359300
  70.9 24.1 %collective-permute-start.1 = (f32[768,256]{0,1:T(8,128)S(1)}, f32[768,256]{0,1:T(8,128)S(1)}, u32[]{:S(2)}, u32[]{:S(2)}) collective-permute-start(f32[768,256]{0,1:T(8,128)S(1)} %constant_dynamic-slice_fusion.1), channel_id=1, source_target_pairs={{0,2},{1,3},{2,0},{3,1},{4,6},{5,7},{6,4},{7,5},{8,10},{9,11},{10,... | collective-permute-start | bytes 2359304 | tf_op jit(solution)/shard_map/ppermute | solution.py:11
  77.0 12.0 %collective-permute-start.10 = (bf16[64,768]{1,0:T(8,128)(2,1)S(1)}, bf16[64,768]{1,0:T(8,128)(2,1)S(1)}, u32[]{:S(2)}, u32[]{:S(2)}) collective-permute-start(bf16[64,768]{1,0:T(8,128)(2,1)S(1)} %fusion.27), channel_id=1, source_target_pairs={{0,2},{1,3},{2,0},{3,1},{4,6},{5,7},{6,4},{7,5},{8,10},{9,11},{10,... | collective-permute-start | bytes 294920 | tf_op jit(solution)/shard_map/ppermute | solution.py:97
  78.3 16.2 %collective-permute-start.11 = (bf16[64,768]{1,0:T(8,128)(2,1)S(1)}, bf16[64,768]{1,0:T(8,128)(2,1)S(1)}, u32[]{:S(2)}, u32[]{:S(2)}) collective-permute-start(bf16[64,768]{1,0:T(8,128)(2,1)S(1)} %fusion.27), channel_id=1, source_target_pairs={{0,3},{1,0},{2,1},{3,2},{4,7},{5,4},{6,5},{7,6},{8,11},{9,8},{10,9... | collective-permute-start | bytes 294920 | tf_op jit(solution)/shard_map/ppermute | solution.py:97
  80.3 14.1 %collective-permute-start.9 = (bf16[64,768]{1,0:T(8,128)(2,1)S(1)}, bf16[64,768]{1,0:T(8,128)(2,1)S(1)}, u32[]{:S(2)}, u32[]{:S(2)}) collective-permute-start(bf16[64,768]{1,0:T(8,128)(2,1)S(1)} %fusion.27), channel_id=1, source_target_pairs={{0,1},{1,2},{2,3},{3,0},{4,5},{5,6},{6,7},{7,4},{8,9},{9,10},{10,1... | collective-permute-start | bytes 294920 | tf_op jit(solution)/shard_map/ppermute | solution.py:97

commit v2 on v1

v2 whole, which is shorter than its diff:
```python
import functools

import jax
import jax.numpy as jnp
from jax import lax
from jax.experimental import pallas as pl
from jax.experimental.pallas import tpu as pltpu
from jax.sharding import PartitionSpec as P

F32 = jnp.float32
BF16 = jnp.bfloat16
MIB = 1024 * 1024
ANY = pl.BlockSpec(memory_space=pl.ANY)
VMEM = pl.BlockSpec(memory_space=pltpu.VMEM)
SMEM = pl.BlockSpec(memory_space=pltpu.SMEM)
DMA = pltpu.SemaphoreType.DMA


def swap(x, axis, size, bit):
    return lax.ppermute(x, axis, [(i, i ^ bit) for i in range(size)])


def shift(x, axis, size, step):
    return lax.ppermute(x, axis, [(i, (i + step) % size) for i in range(size)])


def row_tiles(rows):
    return 3 if rows % 384 == 0 else 1


def base_kernel(bits, tokens, weight, *refs):
    send, keep, held, slots, token_sems, weight_sems = refs[-6:]
    tiles, size = token_sems.shape[0], weight_sems.shape[0]
    half, block = size // 2, slots.shape[2]
    tile = tokens.shape[0] // tiles

    def fetch_tokens(t):
        part = pl.ds(t * tile, tile)
        return pltpu.make_async_copy(tokens.at[part], held.at[part], token_sems.at[t])

    def fetch_weight(m):
        which = bits[0] if m >= half else 1 - bits[0]
        column = pl.multiple_of((2 * (m % half) + which) * block, block)
        return pltpu.make_async_copy(weight.at[:, pl.ds(column, block)], slots.at[m], weight_sems.at[m])

    fetch_tokens(0).start()
    fetch_weight(0).start()
    for t in range(1, tiles):
        fetch_tokens(t).start()
    for m in range(1, size):
        fetch_weight(m).start()
    for m in range(size):
        fetch_weight(m).wait()
        to = keep if m >= half else send
        columns = slice(m % half * block, (m % half + 1) * block)
        for t in range(tiles):
            if m == 0:
                fetch_tokens(t).wait()
            part = slice(t * tile, (t + 1) * tile)
            to[part, columns] = jnp.dot(held[part, :], slots[m], preferred_element_type=F32).astype(to.dtype)


def base_halves(tokens, weight, bit, size, behind=()):
    rows, features = tokens.shape
    block = weight.shape[1] // size
    half = size // 2
    return pl.pallas_call(
        base_kernel,
        in_specs=[SMEM, ANY, ANY] + [ANY] * len(behind),
        out_specs=[VMEM, VMEM],
        out_shape=[jax.ShapeDtypeStruct((rows, half * block), BF16), jax.ShapeDtypeStruct((rows, half * block), F32)],
        scratch_shapes=[
            pltpu.VMEM((rows, features), tokens.dtype),
            pltpu.VMEM((size, features, block), weight.dtype),
            DMA((row_tiles(rows),)),
            DMA((size,)),
        ],
        compiler_params=pltpu.CompilerParams(vmem_limit_bytes=16 * MIB),
        cost_estimate=pl.CostEstimate(
            flops=2 * rows * features * block * size,
            bytes_accessed=2 * features * (rows + block * size),
            transcendentals=0,
        ),
    )(bit.reshape(1).astype(jnp.int32), tokens, weight, *behind)


def pass_kernel(flag, *refs):
    refs[-1][0] = flag[0]


def once(flag, *arrays):
    return pl.pallas_call(
        pass_kernel,
        in_specs=[SMEM] + [ANY] * len(arrays),
        out_specs=SMEM,
        out_shape=jax.ShapeDtypeStruct((1,), jnp.int32),
        compiler_params=pltpu.CompilerParams(vmem_limit_bytes=128 * 1024),
        cost_estimate=pl.CostEstimate(flops=0, bytes_accessed=0, transcendentals=0),
    )(flag.astype(jnp.int32).reshape(1), *arrays)


def make(sizes):
    groups, holders, tensor = sizes["groups"], sizes["adapter"], sizes["tensor"]

    def per_device(tokens, token_adapter_index, adapter_page_index, base_weight, down, up):
        rows, features = tokens.shape
        resident, rank, width = up.shape
        adapters = adapter_page_index.shape[0]
        block = width // tensor
        group, holder, share = lax.axis_index("groups"), lax.axis_index("adapter"), lax.axis_index("tensor")

        onehot = token_adapter_index[:, 0][None, :] == jnp.arange(adapters, dtype=jnp.int32)[:, None]
        page = jnp.sum(jnp.where(onehot, adapter_page_index[:, None], 0), axis=0)

        shared = groups if resident % groups == 0 else 1
        part = resident // shared
        mine = group if shared > 1 else 0
        piece = jnp.concatenate(
            [
                lax.dynamic_slice_in_dim(down, mine * part, part, axis=0).reshape(part * rank, features),
                lax.dynamic_slice(up, (mine * part, 0, share * block), (part, rank, block)).reshape(part * rank, block),
            ],
            axis=1,
        )
        own_up = lax.dynamic_slice_in_dim(up, share * block, block, axis=2).reshape(resident * rank, block)
        pieces = [(down.reshape(resident * rank, features), holder * resident)]
        line = holders == 4 and groups == 2 and tensor == 4
        if line and shared == 2:

            def ends(p):
                return lax.ppermute(p, "adapter", [(1, 0), (2, 3)])

            def middle(p):
                return lax.ppermute(p, "adapter", [(1, 2), (2, 1)])

            def across(p):
                return swap(p, "groups", 2, 1)

            def choose(flag, p, q):
                return jnp.where(flag.reshape(()) == 1, p, q)

            inner = ((holder == 1) | (holder == 2)).astype(jnp.int32)
            near = swap(piece, "adapter", 4, 1)
            mid = middle(piece)
            send, keep = base_halves(tokens, base_weight, share & 1, tensor)
            recv = swap(send, "tensor", tensor, 1)
            high = share // 2

            def pick(which):
                return lax.dynamic_slice_in_dim(keep, which * block, block, axis=1) + lax.dynamic_slice_in_dim(
                    recv, which * block, block, axis=1
                ).astype(F32)

            out, kept = pick(1 - high).astype(BF16), pick(high)
            other = swap(out, "tensor", tensor, 2)
            fout, fmid, ynear = ends(mid), middle(near), across(near)
            far = choose(once(inner, out), mid, fout)
            yfar = across(far)
            ready = once(inner, other, ynear)
            last = choose(ready, fmid, ends(fmid))
            lasts, ylasts = [last], [across(last)]
            base = kept + other.astype(F32)

            def add(source, these, those):
                for found, half in ((these, group), (those, 1 - group)):
                    first = source * resident + half * part
                    for p in found:
                        pieces.append((p, first))
                        first += p.shape[0] // rank

            add(holder ^ 1, [near], [ynear])
            add(jnp.where(inner == 1, holder ^ 3, holder ^ 2), [far], [yfar])
            add(jnp.where(inner == 1, holder ^ 2, holder ^ 3), lasts, ylasts)
        else:
            line = False
            whole = jnp.dot(tokens, base_weight, preferred_element_type=F32)
            base = lax.psum_scatter(whole, "tensor", scatter_dimension=1, tiled=True)
            for step in range(1, holders):
                piece = shift(piece, "adapter", holders, -1)
                source = (holder + step) % holders * resident
                pieces.append((piece, source + mine * part))
                for turn in range(1, shared):
                    pieces.append((shift(piece, "groups", groups, turn), source + (group - turn) % shared * part))

        shrink = jnp.zeros((rank, rows), F32)
        for piece, first in pieces:
            product = lax.dot_general(piece[:, :features], tokens, (((1,), (1,)), ((), ())), preferred_element_type=F32)
            for k in range(piece.shape[0] // rank):
                shrink = shrink + jnp.where(page[None, :] == first + k, product[k * rank : (k + 1) * rank], 0.0)
        shrink = shrink.astype(BF16)
        total = shrink.astype(F32)
        if line:
            total = total + swap(shrink, "tensor", tensor, 1).astype(F32)
            total = total + swap(total.astype(BF16), "tensor", tensor, 2).astype(F32)
        else:
            for step in range(1, tensor):
                total = total + shift(shrink, "tensor", tensor, step).astype(F32)
        total = total.astype(BF16)

        spread = jnp.concatenate(
            [
                jnp.where(page[None, :] == first + k, total, 0)
                for piece, first in pieces
                for k in range(piece.shape[0] // rank)
            ],
            axis=0,
        )
        ups = jnp.concatenate([own_up] + [piece[:, features:] for piece, _ in pieces[1:]], axis=0)
        delta = lax.dot_general(spread, ups, (((0,), (0,)), ((), ())), preferred_element_type=F32)
        return (base + delta).astype(BF16)

    return per_device


def solution(mesh):
    placed = (
        P(("groups", "adapter"), "tensor"),
        P(("groups", "adapter"), None),
        P(),
        P("tensor", None),
        P("adapter", None, "tensor"),
        P("adapter", None, None),
    )
    return jax.shard_map(
        make(dict(mesh.shape)),
        mesh=mesh,
        in_specs=placed,
        out_specs=P(("groups", "adapter"), "tensor"),
        check_vma=False,
    )
```

time: 97 us -> 87.5 us (0.902)
  the two profiles are of different devices: /device:TPU:17 before, /device:TPU:0 now
where the time goes in v2:
time: 87.5 us; the launch traced here: 87 us
  waiting for transfers between devices  32.8 us (37%)
  starting transfers between devices  17 us (19%)
  matrix products  15.2 us (17%)
  local copies, waits for them, and re-layouts  9.29 us (11%)
  Pallas kernels  7.69 us (9%)
  other arithmetic  3.14 us (4%)
  between operations  1.85 us (2%)
    ppermute x2, waiting for transfers between devices, ends(): return lax.ppermute(p, 'adapter', [(1, 0), (2, 3)])  18.6 us
    ppermute x8, waiting for transfers between devices, swap(): return lax.ppermute(x, axis, [(i, i ^ bit) for i in range(size)])  14.2 us
    dot_general x7, matrix products, per_device(): lax.dot_general(piece[:, :features], tokens, (((1,), (1,)), ((), ())), pr...  12.9 us
    ppermute x8, starting transfers between devices, swap(): return lax.ppermute(x, axis, [(i, i ^ bit) for i in range(size)])  12.1 us
    unnamed x22, local copies, waits for them, and re-layouts  7.47 us
    pallas_call x1, Pallas kernels, base_halves(): pl.pallas_call(base_kernel, in_specs=[SMEM, ANY, ANY] + [ANY] * len(behin...  6.65 us
    ppermute x2, starting transfers between devices, ends(): return lax.ppermute(p, 'adapter', [(1, 0), (2, 3)])  2.75 us
    dot_general x1, matrix products, per_device(): lax.dot_general(spread, ups, (((0,), (0,)), ((), ())), preferred_element_...  2.38 us
  transfers between devices with their start and end apart: 12, of which 5 were waited for; matrix products, arithmetic and copies ran while one was open for 19% of the time, Pallas kernels for 9%

profile of v2, /device:TPU:0, one launch (start us, length us, event | category | flops | bytes accessed | tf_op | source)
XLA Modules:
  0.0 87.0 jit_solution(16792851708275885871)
XLA Ops:
  0.0 1.2 %copy-done = bf16[4,64,2048]{2,1,0:T(8,128)(2,1)S(1)} copy-done((bf16[4,64,2048]{2,1,0:T(8,128)(2,1)S(1)}, bf16[4,64,2048]{2,1,0:T(8,128)(2,1)}, u32[]{:S(2)}) %copy-start) | copy-done | bytes 1048600
  1.3 0.9 constant_dynamic-slice_fusion.1
  2.1 0.9 pad_maximum_fusion
  3.0 1.5 %collective-permute-start.4 = (bf16[128,2304]{1,0:T(8,128)(2,1)}, bf16[128,2304]{1,0:T(8,128)(2,1)}, u32[]{:S(2)}, u32[]{:S(2)}) collective-permute-start(bf16[128,2304]{1,0:T(8,128)(2,1)} %pad_maximum_fusion), channel_id=1, source_target_pairs={{4,8},{8,4},{5,9},{9,5},{6,10},{10,6},{7,11},{11,7},{20,24},{24,20... | collective-permute-start | bytes 1769480 | tf_op jit(solution)/shard_map/ppermute | solution.py:134
  4.5 5.1 %collective-permute-start.2 = (bf16[128,2304]{1,0:T(8,128)(2,1)}, bf16[128,2304]{1,0:T(8,128)(2,1)}, u32[]{:S(2)}, u32[]{:S(2)}) collective-permute-start(bf16[128,2304]{1,0:T(8,128)(2,1)} %pad_maximum_fusion), channel_id=1, source_target_pairs={{0,4},{4,0},{8,12},{12,8},{1,5},{5,1},{9,13},{13,9},{2,6},{6,2},{1... | collective-permute-start | bytes 1769480 | tf_op jit(solution)/shard_map/ppermute | solution.py:20
  9.6 1.9 %copy-done.1 = bf16[768,2048]{1,0:T(8,128)(2,1)S(1)} copy-done((bf16[768,2048]{1,0:T(8,128)(2,1)S(1)}, bf16[768,2048]{1,0:T(8,128)(2,1)}, u32[]{:S(2)}) %copy-start.1) | copy-done | bytes 3145752
  11.5 2.2 %copy-done.3 = bf16[2048,1024]{1,0:T(8,128)(2,1)S(1)} copy-done((bf16[2048,1024]{1,0:T(8,128)(2,1)S(1)}, bf16[2048,1024]{1,0:T(8,128)(2,1)}, u32[]{:S(2)}) %copy-start.3) | copy-done | bytes 4194328
  13.6 6.7 %shard_map.64 = (bf16[768,512]{1,0:T(8,128)(2,1)S(1)}, f32[768,512]{1,0:T(8,128)S(1)}) custom-call(s32[1]{0:T(128)} %bitcast.bits, bf16[768,2048]{1,0:T(8,128)(2,1)S(1)} %copy-done.1, bf16[2048,1024]{1,0:T(8,128)(2,1)S(1)} %copy-done.3), custom_call_target="tpu_custom_call" | custom-call | flops 3221225472 | bytes 7340032 | tf_op jit(solution)/shard_map/pallas_call | solution.py:67
  20.3 0.1 collective-permute-start
  20.4 0.9 %constant_dynamic-slice_fusion.2 = bf16[4,64,256]{2,1,0:T(8,128)(2,1)S(1)} fusion(bf16[4,64,1024]{2,1,0:T(8,128)(2,1)} %param.11, s32[]{:T(128)S(6)} %select_n.152), kind=kLoop, calls=%fused_computation.95 | loop fusion | bytes 262148 | tf_op jit(solution)/shard_map/dynamic_slice | solution.py:125
  21.3 0.7 constant_dynamic-update-slice_fusion
  22.0 0.0 copy-start.7
  22.0 3.8 %fusion.29 = f32[256,768]{1,0:T(8,128)} fusion(bf16[256,2048]{1,0:T(8,128)(2,1)S(1)} %bitcast.18, bf16[768,2048]{1,0:T(8,128)(2,1)} %tokens.1), kind=kOutput, calls=%fused_computation.96 | convolution fusion | flops 805306368 | bytes 4980736 | tf_op jit(solution)/shard_map/dot_general | solution.py:187
  25.8 0.1 select_reduce_fusion
  26.0 0.0 collective-permute-done.2
  26.0 1.6 %collective-permute-start.3 = (bf16[128,2304]{1,0:T(8,128)(2,1)}, bf16[128,2304]{1,0:T(8,128)(2,1)S(1)}, u32[]{:S(2)}, u32[]{:S(2)}) collective-permute-start(bf16[128,2304]{1,0:T(8,128)(2,1)} %collective-permute-done.2), channel_id=1, source_target_pairs={{0,16},{16,0},{1,17},{17,1},{2,18},{18,2},{3,19},{19,3},{4,20},{20... | collective-permute-start | bytes 1769480 | tf_op jit(solution)/shard_map/ppermute | solution.py:20
  27.6 0.7 collective-permute-start.7
  28.3 0.0 collective-permute-done.4
  28.3 1.3 %collective-permute-start.5 = (bf16[128,2304]{1,0:T(8,128)(2,1)}, bf16[128,2304]{1,0:T(8,128)(2,1)S(1)}, u32[]{:S(2)}, u32[]{:S(2)}) collective-permute-start(bf16[128,2304]{1,0:T(8,128)(2,1)} %collective-permute-done.4), channel_id=1, source_target_pairs={{4,0},{8,12},{5,1},{9,13},{6,2},{10,14},{7,3},{11,15},{20,16},{24,... | collective-permute-start | bytes 1769480 | tf_op jit(solution)/shard_map/ppermute | solution.py:131
  29.6 1.5 %slice_dynamic-update-slice_fusion.5 = bf16[1024,256]{1,0:T(8,128)(2,1)} fusion(bf16[1024,256]{1,0:T(8,128)(2,1)} %constant_dynamic-update-slice_fusion, bf16[128,2304]{1,0:T(8,128)(2,1)} %collective-permute-done.2), kind=kLoop, calls=%fused_computation.73 | loop fusion | bytes 131072
  31.1 3.2 %fusion.10 = f32[128,768]{1,0:T(8,128)S(1)} fusion(bf16[768,2048]{1,0:T(8,128)(2,1)} %tokens.1, bf16[128,2304]{1,0:T(8,128)(2,1)} %collective-permute-done.2), kind=kOutput, calls=%fused_computation.15 | convolution fusion | flops 402653184 | bytes 4063232 | tf_op jit(solution)/shard_map/dot_general | solution.py:187
  34.3 0.0 collective-permute-done
  34.3 0.0 copy-start.2
  34.3 1.3 %add_convert_fusion.1.refs_0_ = bf16[768,256]{1,0:T(8,128)(2,1)S(1)} fusion(f32[768,512]{1,0:T(8,128)S(1)} %get-tuple-element.7, s32[]{:T(128)S(6)} %select_n.145, bf16[768,512]{1,0:T(8,128)(2,1)} %collective-permute-done), kind=kLoop, calls=%fused_computation.1 | loop fusion | flops 589824 | bytes 1572868 | tf_op jit(solution)/shard_map/convert_element_type | solution.py:154
  35.6 1.6 %collective-permute-start.1 = (bf16[768,256]{1,0:T(8,128)(2,1)S(1)}, bf16[768,256]{1,0:T(8,128)(2,1)S(1)}, u32[]{:S(2)}, u32[]{:S(2)}) collective-permute-start(bf16[768,256]{1,0:T(8,128)(2,1)S(1)} %add_convert_fusion.1.refs_0_), channel_id=1, source_target_pairs={{0,2},{1,3},{2,0},{3,1},{4,6},{5,7},{6,4},{7,5},{8,10},{9,11},{10,... | collective-permute-start | bytes 1179656 | tf_op jit(solution)/shard_map/ppermute | solution.py:20
  37.2 0.5 shard_map.65
  38.4 7.5 %collective-permute-done.5 = bf16[128,2304]{1,0:T(8,128)(2,1)S(1)} collective-permute-done((bf16[128,2304]{1,0:T(8,128)(2,1)}, bf16[128,2304]{1,0:T(8,128)(2,1)S(1)}, u32[]{:S(2)}, u32[]{:S(2)}) %collective-permute-start.5) | collective-permute-done | bytes 589856 | tf_op jit(solution)/shard_map/ppermute | solution.py:131
  45.9 0.1 broadcast_select_fusion.1
  46.0 0.6 collective-permute-start.6
  46.5 1.5 %collective-permute-start.8 = (bf16[128,2304]{1,0:T(8,128)(2,1)S(1)}, bf16[128,2304]{1,0:T(8,128)(2,1)S(1)}, u32[]{:S(2)}, u32[]{:S(2)}) collective-permute-start(bf16[128,2304]{1,0:T(8,128)(2,1)S(1)} %collective-permute-done.7), channel_id=1, source_target_pairs={{4,0},{8,12},{5,1},{9,13},{6,2},{10,14},{7,3},{11,15},{20,16},{24,... | collective-permute-start | bytes 1769480 | tf_op jit(solution)/shard_map/ppermute | solution.py:131
  48.0 1.2 %fusion.6 = f32[128,768]{1,0:T(8,128)S(1)} fusion(bf16[768,2048]{1,0:T(8,128)(2,1)S(1)} %copy-done.2, bf16[128,2304]{1,0:T(8,128)(2,1)S(1)} %broadcast_select_fusion.1), kind=kOutput, calls=%fused_computation.11 | convolution fusion | flops 402653184 | bytes 4063232 | tf_op jit(solution)/shard_map/dot_general | solution.py:187
  49.2 0.0 collective-permute-done.1.refs_0_
  49.2 0.5 shard_map.66
  50.5 1.2 %fusion.8 = f32[128,768]{1,0:T(8,128)S(1)} fusion(bf16[768,2048]{1,0:T(8,128)(2,1)S(1)} %copy-done.2, bf16[128,2304]{1,0:T(8,128)(2,1)S(1)} %collective-permute-done.3.refs_1_), kind=kOutput, calls=%fused_computation.13 | convolution fusion | flops 402653184 | bytes 4063232 | tf_op jit(solution)/shard_map/dot_general | solution.py:187
  51.6 11.1 %collective-permute-done.8 = bf16[128,2304]{1,0:T(8,128)(2,1)S(1)} collective-permute-done((bf16[128,2304]{1,0:T(8,128)(2,1)S(1)}, bf16[128,2304]{1,0:T(8,128)(2,1)S(1)}, u32[]{:S(2)}, u32[]{:S(2)}) %collective-permute-start.8) | collective-permute-done | bytes 589856 | tf_op jit(solution)/shard_map/ppermute | solution.py:131
  62.8 0.1 broadcast_select_fusion
  62.8 1.6 %collective-permute-start.9 = (bf16[128,2304]{1,0:T(8,128)(2,1)S(1)}, bf16[128,2304]{1,0:T(8,128)(2,1)S(1)}, u32[]{:S(2)}, u32[]{:S(2)}) collective-permute-start(bf16[128,2304]{1,0:T(8,128)(2,1)S(1)} %broadcast_select_fusion), channel_id=1, source_target_pairs={{0,16},{16,0},{1,17},{17,1},{2,18},{18,2},{3,19},{19,3},{4,20},{20... | collective-permute-start | bytes 1769480 | tf_op jit(solution)/shard_map/ppermute | solution.py:20
  64.4 1.2 %fusion.2 = f32[128,768]{1,0:T(8,128)S(1)} fusion(bf16[768,2048]{1,0:T(8,128)(2,1)S(1)} %copy-done.2, bf16[128,2304]{1,0:T(8,128)(2,1)S(1)} %broadcast_select_fusion), kind=kOutput, calls=%fused_computation.7 | convolution fusion | flops 402653184 | bytes 4063232 | tf_op jit(solution)/shard_map/dot_general | solution.py:187
  65.6 1.2 %fusion.4 = f32[128,768]{1,0:T(8,128)S(1)} fusion(bf16[768,2048]{1,0:T(8,128)(2,1)S(1)} %copy-done.2, bf16[128,2304]{1,0:T(8,128)(2,1)S(1)} %collective-permute-done.6), kind=kOutput, calls=%fused_computation.9 | convolution fusion | flops 402653184 | bytes 4063232 | tf_op jit(solution)/shard_map/dot_general | solution.py:187
  66.8 9.5 %collective-permute-done.9 = bf16[128,2304]{1,0:T(8,128)(2,1)S(1)} collective-permute-done((bf16[128,2304]{1,0:T(8,128)(2,1)S(1)}, bf16[128,2304]{1,0:T(8,128)(2,1)S(1)}, u32[]{:S(2)}, u32[]{:S(2)}) %collective-permute-start.9) | collective-permute-done | bytes 589856 | tf_op jit(solution)/shard_map/ppermute | solution.py:20
  76.3 1.2 %fusion = f32[128,768]{1,0:T(8,128)S(1)} fusion(bf16[768,2048]{1,0:T(8,128)(2,1)S(1)} %copy-done.2, bf16[128,2304]{1,0:T(8,128)(2,1)S(1)} %collective-permute-done.9), kind=kOutput, calls=%fused_computation.5 | convolution fusion | flops 402653184 | bytes 4063232 | tf_op jit(solution)/shard_map/dot_general | solution.py:187
  77.5 0.3 fusion.13
  77.8 0.1 collective-permute-start.10
  77.9 1.3 %collective-permute-done.10 = bf16[64,768]{1,0:T(8,128)(2,1)S(1)} collective-permute-done((bf16[64,768]{1,0:T(8,128)(2,1)S(1)}, bf16[64,768]{1,0:T(8,128)(2,1)S(1)}, u32[]{:S(2)}, u32[]{:S(2)}) %collective-permute-start.10) | collective-permute-done | bytes 98336 | tf_op jit(solution)/shard_map/ppermute | solution.py:20
  79.2 1.5 %collective-permute-start.11 = (bf16[64,768]{1,0:T(8,128)(2,1)S(1)}, bf16[64,768]{1,0:T(8,128)(2,1)S(1)}, u32[]{:S(2)}, u32[]{:S(2)}) collective-permute-start(bf16[64,768]{1,0:T(8,128)(2,1)S(1)} %fusion.28), channel_id=1, source_target_pairs={{0,2},{1,3},{2,0},{3,1},{4,6},{5,7},{6,4},{7,5},{8,10},{9,11},{10,... | collective-permute-start | bytes 294920 | tf_op jit(solution)/shard_map/ppermute | solution.py:20
  80.7 3.4 %collective-permute-done.11 = bf16[64,768]{1,0:T(8,128)(2,1)S(1)} collective-permute-done((bf16[64,768]{1,0:T(8,128)(2,1)S(1)}, bf16[64,768]{1,0:T(8,128)(2,1)S(1)}, u32[]{:S(2)}, u32[]{:S(2)}) %collective-permute-start.11) | collective-permute-done | bytes 98336 | tf_op jit(solution)/shard_map/ppermute | solution.py:20
  84.1 0.1 select_dynamic-update-slice_fusion.15
  84.6 2.4 %add_convert_fusion = bf16[768,256]{1,0:T(8,128)(2,1)} fusion(bf16[768,256]{1,0:T(8,128)(2,1)S(1)} %collective-permute-done.1.refs_0_, f32[768,512]{1,0:T(8,128)S(1)} %get-tuple-element.7, s32[]{:T(128)S(6)} %select_n.144, bf16[768,512]{1,0:T(8,128)(2,1)} %collective-permute-done, bf16[1024,768]{1,0:T(8,128)(2,1)S(1)} %select_dynamic-update-slice_fusion, ...), kind=kOutput, calls=%fused_computation | convolution fusion | flops 403832832 | bytes 4063236 | tf_op jit(solution)/shard_map/dot_general | solution.py:209
  (38 shorter events, 0.5 us)
Async XLA Ops:
  0.0 1.2 %copy-start = (bf16[4,64,2048]{2,1,0:T(8,128)(2,1)S(1)}, bf16[4,64,2048]{2,1,0:T(8,128)(2,1)}, u32[]{:S(2)}) copy-start(bf16[4,64,2048]{2,1,0:T(8,128)(2,1)} %param.10) | copy-start | bytes 3145732
  3.0 25.3 %collective-permute-start.4 = (bf16[128,2304]{1,0:T(8,128)(2,1)}, bf16[128,2304]{1,0:T(8,128)(2,1)}, u32[]{:S(2)}, u32[]{:S(2)}) collective-permute-start(bf16[128,2304]{1,0:T(8,128)(2,1)} %pad_maximum_fusion), channel_id=1, source_target_pairs={{4,8},{8,4},{5,9},{9,5},{6,10},{10,6},{7,11},{11,7},{20,24},{24,20... | collective-permute-start | bytes 1769480 | tf_op jit(solution)/shard_map/ppermute | solution.py:134
  4.5 21.5 %collective-permute-start.2 = (bf16[128,2304]{1,0:T(8,128)(2,1)}, bf16[128,2304]{1,0:T(8,128)(2,1)}, u32[]{:S(2)}, u32[]{:S(2)}) collective-permute-start(bf16[128,2304]{1,0:T(8,128)(2,1)} %pad_maximum_fusion), channel_id=1, source_target_pairs={{0,4},{4,0},{8,12},{12,8},{1,5},{5,1},{9,13},{13,9},{2,6},{6,2},{1... | collective-permute-start | bytes 1769480 | tf_op jit(solution)/shard_map/ppermute | solution.py:20
  9.6 1.9 %copy-start.1 = (bf16[768,2048]{1,0:T(8,128)(2,1)S(1)}, bf16[768,2048]{1,0:T(8,128)(2,1)}, u32[]{:S(2)}) copy-start(bf16[768,2048]{1,0:T(8,128)(2,1)} %tokens.1) | copy-start | bytes 9437188
  11.5 2.2 %copy-start.3 = (bf16[2048,1024]{1,0:T(8,128)(2,1)S(1)}, bf16[2048,1024]{1,0:T(8,128)(2,1)}, u32[]{:S(2)}) copy-start(bf16[2048,1024]{1,0:T(8,128)(2,1)} %weight.1) | copy-start | bytes 12582916
  13.6 8.3 %copy-start.6 = (s32[768,1]{0,1:T(1,128)S(1)}, s32[768,1]{0,1:T(1,128)}, u32[]{:S(2)}) copy-start(s32[768,1]{0,1:T(1,128)} %param.7) | copy-start | bytes 9220
  20.3 14.0 %collective-permute-start = (bf16[768,512]{1,0:T(8,128)(2,1)S(1)}, bf16[768,512]{1,0:T(8,128)(2,1)}, u32[]{:S(2)}, u32[]{:S(2)}) collective-permute-start(bf16[768,512]{1,0:T(8,128)(2,1)S(1)} %get-tuple-element.8), channel_id=1, source_target_pairs={{0,1},{1,0},{2,3},{3,2},{4,5},{5,4},{6,7},{7,6},{8,9},{9,8},{10,11... | collective-permute-start | bytes 2359304 | tf_op jit(solution)/shard_map/ppermute | solution.py:20
  22.0 3.8 %copy-start.7 = (s32[16]{0:T(128)S(1)}, s32[16]{0:T(128)}, u32[]{:S(2)}) copy-start(s32[16]{0:T(128)} %param.8) | copy-start | bytes 196
  26.0 23.2 %collective-permute-start.3 = (bf16[128,2304]{1,0:T(8,128)(2,1)}, bf16[128,2304]{1,0:T(8,128)(2,1)S(1)}, u32[]{:S(2)}, u32[]{:S(2)}) collective-permute-start(bf16[128,2304]{1,0:T(8,128)(2,1)} %collective-permute-done.2), channel_id=1, source_target_pairs={{0,16},{16,0},{1,17},{17,1},{2,18},{18,2},{3,19},{19,3},{4,20},{20... | collective-permute-start | bytes 1769480 | tf_op jit(solution)/shard_map/ppermute | solution.py:20
  27.6 18.9 %collective-permute-start.7 = (bf16[128,2304]{1,0:T(8,128)(2,1)}, bf16[128,2304]{1,0:T(8,128)(2,1)S(1)}, u32[]{:S(2)}, u32[]{:S(2)}) collective-permute-start(bf16[128,2304]{1,0:T(8,128)(2,1)} %collective-permute-done.2), channel_id=1, source_target_pairs={{4,8},{8,4},{5,9},{9,5},{6,10},{10,6},{7,11},{11,7},{20,24},{24,20... | collective-permute-start | bytes 1769480 | tf_op jit(solution)/shard_map/ppermute | solution.py:134
  28.3 17.6 %collective-permute-start.5 = (bf16[128,2304]{1,0:T(8,128)(2,1)}, bf16[128,2304]{1,0:T(8,128)(2,1)S(1)}, u32[]{:S(2)}, u32[]{:S(2)}) collective-permute-start(bf16[128,2304]{1,0:T(8,128)(2,1)} %collective-permute-done.4), channel_id=1, source_target_pairs={{4,0},{8,12},{5,1},{9,13},{6,2},{10,14},{7,3},{11,15},{20,16},{24,... | collective-permute-start | bytes 1769480 | tf_op jit(solution)/shard_map/ppermute | solution.py:131
  34.3 13.7 %copy-start.2 = (bf16[768,2048]{1,0:T(8,128)(2,1)S(1)}, bf16[768,2048]{1,0:T(8,128)(2,1)}, u32[]{:S(2)}) copy-start(bf16[768,2048]{1,0:T(8,128)(2,1)} %tokens.1) | copy-start | bytes 9437188
  35.6 13.6 %collective-permute-start.1 = (bf16[768,256]{1,0:T(8,128)(2,1)S(1)}, bf16[768,256]{1,0:T(8,128)(2,1)S(1)}, u32[]{:S(2)}, u32[]{:S(2)}) collective-permute-start(bf16[768,256]{1,0:T(8,128)(2,1)S(1)} %add_convert_fusion.1.refs_0_), channel_id=1, source_target_pairs={{0,2},{1,3},{2,0},{3,1},{4,6},{5,7},{6,4},{7,5},{8,10},{9,11},{10,... | collective-permute-start | bytes 1179656 | tf_op jit(solution)/shard_map/ppermute | solution.py:20
  45.9 3.2 %copy-start.5 = (bf16[1024,256]{1,0:T(8,128)(2,1)S(1)}, bf16[1024,256]{1,0:T(8,128)(2,1)}, u32[]{:S(2)}) copy-start(bf16[1024,256]{1,0:T(8,128)(2,1)} %slice_dynamic-update-slice_fusion.5) | copy-start | bytes 1572868
  46.0 19.6 %collective-permute-start.6 = (bf16[128,2304]{1,0:T(8,128)(2,1)S(1)}, bf16[128,2304]{1,0:T(8,128)(2,1)S(1)}, u32[]{:S(2)}, u32[]{:S(2)}) collective-permute-start(bf16[128,2304]{1,0:T(8,128)(2,1)S(1)} %broadcast_select_fusion.1), channel_id=1, source_target_pairs={{0,16},{16,0},{1,17},{17,1},{2,18},{18,2},{3,19},{19,3},{4,20},{20... | collective-permute-start | bytes 1769480 | tf_op jit(solution)/shard_map/ppermute | solution.py:20
  46.5 16.2 %collective-permute-start.8 = (bf16[128,2304]{1,0:T(8,128)(2,1)S(1)}, bf16[128,2304]{1,0:T(8,128)(2,1)S(1)}, u32[]{:S(2)}, u32[]{:S(2)}) collective-permute-start(bf16[128,2304]{1,0:T(8,128)(2,1)S(1)} %collective-permute-done.7), channel_id=1, source_target_pairs={{4,0},{8,12},{5,1},{9,13},{6,2},{10,14},{7,3},{11,15},{20,16},{24,... | collective-permute-start | bytes 1769480 | tf_op jit(solution)/shard_map/ppermute | solution.py:131
  62.8 13.5 %collective-permute-start.9 = (bf16[128,2304]{1,0:T(8,128)(2,1)S(1)}, bf16[128,2304]{1,0:T(8,128)(2,1)S(1)}, u32[]{:S(2)}, u32[]{:S(2)}) collective-permute-start(bf16[128,2304]{1,0:T(8,128)(2,1)S(1)} %broadcast_select_fusion), channel_id=1, source_target_pairs={{0,16},{16,0},{1,17},{17,1},{2,18},{18,2},{3,19},{19,3},{4,20},{20... | collective-permute-start | bytes 1769480 | tf_op jit(solution)/shard_map/ppermute | solution.py:20
  66.8 10.7 %copy-start.4 = (f32[256,768]{1,0:T(8,128)S(1)}, f32[256,768]{1,0:T(8,128)}, u32[]{:S(2)}) copy-start(f32[256,768]{1,0:T(8,128)} %fusion.29) | copy-start | bytes 2359300
  77.8 1.4 %collective-permute-start.10 = (bf16[64,768]{1,0:T(8,128)(2,1)S(1)}, bf16[64,768]{1,0:T(8,128)(2,1)S(1)}, u32[]{:S(2)}, u32[]{:S(2)}) collective-permute-start(bf16[64,768]{1,0:T(8,128)(2,1)S(1)} %fusion.13), channel_id=1, source_target_pairs={{0,1},{1,0},{2,3},{3,2},{4,5},{5,4},{6,7},{7,6},{8,9},{9,8},{10,11... | collective-permute-start | bytes 294920 | tf_op jit(solution)/shard_map/ppermute | solution.py:20
  79.2 4.9 %collective-permute-start.11 = (bf16[64,768]{1,0:T(8,128)(2,1)S(1)}, bf16[64,768]{1,0:T(8,128)(2,1)S(1)}, u32[]{:S(2)}, u32[]{:S(2)}) collective-permute-start(bf16[64,768]{1,0:T(8,128)(2,1)S(1)} %fusion.28), channel_id=1, source_target_pairs={{0,2},{1,3},{2,0},{3,1},{4,6},{5,7},{6,4},{7,5},{8,10},{9,11},{10,... | collective-permute-start | bytes 294920 | tf_op jit(solution)/shard_map/ppermute | solution.py:20

commit v3 on v2

--- a/solution.py
+++ b/solution.py
@@ -8,12 +8,13 @@
 from jax.sharding import PartitionSpec as P
 
 F32 = jnp.float32
+MIB = 1024 * 1024
+VMEM = pl.BlockSpec(memory_space=pltpu.VMEM)
+DMA = pltpu.SemaphoreType.DMA
+NO_COST = pl.CostEstimate(flops=0, bytes_accessed=0, transcendentals=0)
 BF16 = jnp.bfloat16
-MIB = 1024 * 1024
 ANY = pl.BlockSpec(memory_space=pl.ANY)
-VMEM = pl.BlockSpec(memory_space=pltpu.VMEM)
 SMEM = pl.BlockSpec(memory_space=pltpu.SMEM)
-DMA = pltpu.SemaphoreType.DMA
 
 
 def swap(x, axis, size, bit):
@@ -22,66 +23,6 @@
 
 def shift(x, axis, size, step):
     return lax.ppermute(x, axis, [(i, (i + step) % size) for i in range(size)])
-
-
-def row_tiles(rows):
-    return 3 if rows % 384 == 0 else 1
-
-
-def base_kernel(bits, tokens, weight, *refs):
-    send, keep, held, slots, token_sems, weight_sems = refs[-6:]
-    tiles, size = token_sems.shape[0], weight_sems.shape[0]
-    half, block = size // 2, slots.shape[2]
-    tile = tokens.shape[0] // tiles
-
-    def fetch_tokens(t):
-        part = pl.ds(t * tile, tile)
-        return pltpu.make_async_copy(tokens.at[part], held.at[part], token_sems.at[t])
-
-    def fetch_weight(m):
-        which = bits[0] if m >= half else 1 - bits[0]
-        column = pl.multiple_of((2 * (m % half) + which) * block, block)
-        return pltpu.make_async_copy(weight.at[:, pl.ds(column, block)], slots.at[m], weight_sems.at[m])
-
-    fetch_tokens(0).start()
-    fetch_weight(0).start()
-    for t in range(1, tiles):
-        fetch_tokens(t).start()
-    for m in range(1, size):
-        fetch_weight(m).start()
-    for m in range(size):
-        fetch_weight(m).wait()
-        to = keep if m >= half else send
-        columns = slice(m % half * block, (m % half + 1) * block)
-        for t in range(tiles):
-            if m == 0:
-                fetch_tokens(t).wait()
-            part = slice(t * tile, (t + 1) * tile)
-            to[part, columns] = jnp.dot(held[part, :], slots[m], preferred_element_type=F32).astype(to.dtype)
-
-
-def base_halves(tokens, weight, bit, size, behind=()):
-    rows, features = tokens.shape
-    block = weight.shape[1] // size
-    half = size // 2
-    return pl.pallas_call(
-        base_kernel,
-        in_specs=[SMEM, ANY, ANY] + [ANY] * len(behind),
-        out_specs=[VMEM, VMEM],
-        out_shape=[jax.ShapeDtypeStruct((rows, half * block), BF16), jax.ShapeDtypeStruct((rows, half * block), F32)],
-        scratch_shapes=[
-            pltpu.VMEM((rows, features), tokens.dtype),
-            pltpu.VMEM((size, features, block), weight.dtype),
-            DMA((row_tiles(rows),)),
-            DMA((size,)),
-        ],
-        compiler_params=pltpu.CompilerParams(vmem_limit_bytes=16 * MIB),
-        cost_estimate=pl.CostEstimate(
-            flops=2 * rows * features * block * size,
-            bytes_accessed=2 * features * (rows + block * size),
-            transcendentals=0,
-        ),
-    )(bit.reshape(1).astype(jnp.int32), tokens, weight, *behind)
 
 
 def pass_kernel(flag, *refs):
@@ -95,8 +36,71 @@
         out_specs=SMEM,
         out_shape=jax.ShapeDtypeStruct((1,), jnp.int32),
         compiler_params=pltpu.CompilerParams(vmem_limit_bytes=128 * 1024),
-        cost_estimate=pl.CostEstimate(flops=0, bytes_accessed=0, transcendentals=0),
+        cost_estimate=NO_COST,
     )(flag.astype(jnp.int32).reshape(1), *arrays)
+
+
+def many_kernel(rank, count, numbers, page, tokens, *refs):
+    pieces = refs[:count]
+    acc, held, weights, token_sems, piece_sems = refs[-5:]
+    before = refs[count] if len(refs) == count + 6 else None
+    tiles = token_sems.shape[0]
+    tile = tokens.shape[0] // tiles
+    features = tokens.shape[1]
+
+    def fetch_tokens(t):
+        part = pl.ds(t * tile, tile)
+        return pltpu.make_async_copy(tokens.at[part], held.at[part], token_sems.at[t])
+
+    copies, named, first = [], [], 0
+    for k, p in enumerate(pieces):
+        here = pl.ds(first, p.shape[0])
+        copies.append(pltpu.make_async_copy(p.at[:, pl.ds(0, features)], weights.at[here], piece_sems.at[k]))
+        first += p.shape[0]
+        named += [numbers[k] + j for j in range(p.shape[0] // rank)]
+    fetch_tokens(0).start()
+    for copy in copies:
+        copy.start()
+    for t in range(1, tiles):
+        fetch_tokens(t).start()
+    for copy in copies:
+        copy.wait()
+    chunk = 256 if weights.shape[0] % 256 == 0 else 128 if weights.shape[0] % 128 == 0 else weights.shape[0]
+    for t in range(tiles):
+        fetch_tokens(t).wait()
+        part = slice(t * tile, (t + 1) * tile)
+        pages = page[:, part]
+        total = jnp.zeros((rank, tile), F32) if before is None else before[:, part]
+        for c in range(0, weights.shape[0], chunk):
+            product = lax.dot_general(
+                weights[c : c + chunk, :], held[part, :], (((1,), (1,)), ((), ())), preferred_element_type=F32
+            )
+            for j in range(chunk // rank):
+                mine = pages == named[c // rank + j]
+                total = total + jnp.where(mine, product[j * rank : (j + 1) * rank], 0.0)
+        acc[:, part] = total
+
+
+def shrink_many(tokens, page, pieces, rank, before=None):
+    rows, features = tokens.shape
+    numbers = jnp.stack([first for _, first in pieces]).astype(jnp.int32)
+    weights = [p for p, _ in pieces]
+    tiles = 3 if rows % 384 == 0 else 1
+    earlier = [] if before is None else [before]
+    return pl.pallas_call(
+        functools.partial(many_kernel, rank, len(weights)),
+        in_specs=[SMEM, VMEM, ANY] + [ANY] * len(weights) + [VMEM] * len(earlier),
+        out_specs=VMEM,
+        out_shape=jax.ShapeDtypeStruct((rank, rows), F32),
+        scratch_shapes=[
+            pltpu.VMEM((rows, features), tokens.dtype),
+            pltpu.VMEM((sum(w.shape[0] for w in weights), features), weights[0].dtype),
+            DMA((tiles,)),
+            DMA((len(weights),)),
+        ],
+        compiler_params=pltpu.CompilerParams(vmem_limit_bytes=12 * MIB),
+        cost_estimate=NO_COST,
+    )(numbers, page, tokens, *weights, *earlier)
 
 
 def make(sizes):
@@ -142,25 +146,23 @@
             inner = ((holder == 1) | (holder == 2)).astype(jnp.int32)
             near = swap(piece, "adapter", 4, 1)
             mid = middle(piece)
-            send, keep = base_halves(tokens, base_weight, share & 1, tensor)
+            whole = jnp.dot(tokens, base_weight, preferred_element_type=F32)
+            low, high = share % 2, share // 2
+
+            def columns(a, *starts):
+                return jnp.concatenate([lax.dynamic_slice_in_dim(a, m * block, block, axis=1) for m in starts], axis=1)
+
+            send = columns(whole, 1 - low, 3 - low).astype(BF16)
             recv = swap(send, "tensor", tensor, 1)
-            high = share // 2
 
             def pick(which):
-                return lax.dynamic_slice_in_dim(keep, which * block, block, axis=1) + lax.dynamic_slice_in_dim(
-                    recv, which * block, block, axis=1
-                ).astype(F32)
+                return columns(whole, 2 * which + low) + columns(recv, which).astype(F32)
 
             out, kept = pick(1 - high).astype(BF16), pick(high)
             other = swap(out, "tensor", tensor, 2)
             fout, fmid, ynear = ends(mid), middle(near), across(near)
             far = choose(once(inner, out), mid, fout)
             yfar = across(far)
-            ready = once(inner, other, ynear)
-            last = choose(ready, fmid, ends(fmid))
-            lasts, ylasts = [last], [across(last)]
-            base = kept + other.astype(F32)
-
             def add(source, these, those):
                 for found, half in ((these, group), (those, 1 - group)):
                     first = source * resident + half * part
@@ -169,6 +171,14 @@
                         first += p.shape[0] // rank
 
             add(holder ^ 1, [near], [ynear])
+            first_acc = shrink_many(tokens, page[None, :], pieces, rank)
+            pieces_done = len(pieces)
+            ready = once(inner, other)
+            cut = part * rank // 2
+            halves = lax.optimization_barrier((fmid[:cut], fmid[cut:]))
+            lasts = [choose(ready, p, ends(p)) for p in halves]
+            ylasts = [across(p) for p in lasts]
+            base = kept + other.astype(F32)
             add(jnp.where(inner == 1, holder ^ 3, holder ^ 2), [far], [yfar])
             add(jnp.where(inner == 1, holder ^ 2, holder ^ 3), lasts, ylasts)
         else:
@@ -182,8 +192,11 @@
                 for turn in range(1, shared):
                     pieces.append((shift(piece, "groups", groups, turn), source + (group - turn) % shared * part))
 
-        shrink = jnp.zeros((rank, rows), F32)
-        for piece, first in pieces:
+        shrink, rest = jnp.zeros((rank, rows), F32), pieces
+        if line:
+            shrink = shrink_many(tokens, page[None, :], pieces[pieces_done:-2], rank, first_acc)
+            rest = pieces[-2:]
+        for piece, first in rest:
             product = lax.dot_general(piece[:, :features], tokens, (((1,), (1,)), ((), ())), preferred_element_type=F32)
             for k in range(piece.shape[0] // rank):
                 shrink = shrink + jnp.where(page[None, :] == first + k, product[k * rank : (k + 1) * rank], 0.0)

time: 87.5 us -> 74.8 us (0.85)
  local copies, waits for them, and re-layouts: 9.29 us -> 4.16 us
  matrix products: 15.2 us -> 10.9 us
  waiting for transfers between devices: 32.8 us -> 30.9 us
  starting transfers between devices: 17 us -> 15.4 us
  Pallas kernels: 7.69 us -> 9.09 us
    dot_general x7 -> x2, matrix products: 12.9 us -> 2.17 us  [per_device(): lax.dot_general(piece[:, :features], tokens, (((1,), (1,)), ((), ())), pr...]
    dot_general x0 -> x1, matrix products: none -> 6.13 us  [per_device(): whole = jnp.dot(tokens, base_weight, preferred_element_type=F32)]
    unnamed x22, local copies, waits for them, and re-layouts: 7.47 us -> 2.82 us
    ppermute x8 -> x9, starting transfers between devices: 12.1 us -> 9.07 us  [swap(): return lax.ppermute(x, axis, [(i, i ^ bit) for i in range(size)])]
    ppermute x2 -> x3, waiting for transfers between devices: 18.6 us -> 16.4 us  [ends(): return lax.ppermute(p, 'adapter', [(1, 0), (2, 3)])]
    pallas_call x1 -> x2, Pallas kernels: 6.65 us -> 8.05 us  [shrink_many(): pl.pallas_call(functools.partial(many_kernel, rank, len(weights)), in_spe...]
    ppermute x2 -> x3, starting transfers between devices: 2.75 us -> 4.13 us  [ends(): return lax.ppermute(p, 'adapter', [(1, 0), (2, 3)])]
    dynamic_slice x1, local copies, waits for them, and re-layouts: 0.04 us -> 1.14 us  [per_device(): lax.dynamic_slice_in_dim(down, mine * part, part, axis=0)]
  transfers between devices with their start and end apart: 12 -> 14, of which waited for: 5 -> 8; matrix products, arithmetic and copies ran while one was open for 19% -> 14% of each run, Pallas kernels for 9% -> 12%
where the time goes in v3:
time: 74.8 us; the launch traced here: 74.5 us
  waiting for transfers between devices  30.9 us (41%)
  starting transfers between devices  15.4 us (21%)
  matrix products  10.9 us (15%)
  Pallas kernels  9.09 us (12%)
  local copies, waits for them, and re-layouts  4.16 us (6%)
  other arithmetic  2.36 us (3%)
  between operations  1.74 us (2%)
    ppermute x3, waiting for transfers between devices, ends(): return lax.ppermute(p, 'adapter', [(1, 0), (2, 3)])  16.4 us
    ppermute x9, waiting for transfers between devices, swap(): return lax.ppermute(x, axis, [(i, i ^ bit) for i in range(size)])  14.5 us
    ppermute x9, starting transfers between devices, swap(): return lax.ppermute(x, axis, [(i, i ^ bit) for i in range(size)])  9.07 us
    pallas_call x2, Pallas kernels, shrink_many(): pl.pallas_call(functools.partial(many_kernel, rank, len(weights)), in_spe...  8.05 us
    dot_general x1, matrix products, per_device(): whole = jnp.dot(tokens, base_weight, preferred_element_type=F32)  6.13 us
    ppermute x3, starting transfers between devices, ends(): return lax.ppermute(p, 'adapter', [(1, 0), (2, 3)])  4.13 us
    unnamed x22, local copies, waits for them, and re-layouts  2.82 us
    dot_general x1, matrix products, per_device(): lax.dot_general(spread, ups, (((0,), (0,)), ((), ())), preferred_element_...  2.62 us
  transfers between devices with their start and end apart: 14, of which 8 were waited for; matrix products, arithmetic and copies ran while one was open for 14% of the time, Pallas kernels for 12%

profile of v3, /device:TPU:0, one launch (start us, length us, event | category | flops | bytes accessed | tf_op | source)
XLA Modules:
  0.0 74.5 jit_solution(15878050044938931598)
XLA Ops:
  0.0 1.1 %constant_dynamic-slice_fusion.2 = bf16[2,64,2048]{2,1,0:T(8,128)(2,1)S(1)} fusion(bf16[4,64,2048]{2,1,0:T(8,128)(2,1)} %param.10, s32[]{:T(128)S(6)} %select_n.135), kind=kLoop, calls=%fused_computation.46 | loop fusion | bytes 1048580 | tf_op jit(solution)/shard_map/dynamic_slice | solution.py:124
  1.1 0.1 copy-done
  1.3 3.1 %collective-permute-start.5 = (bf16[128,2304]{1,0:T(8,128)(2,1)S(1)}, bf16[128,2304]{1,0:T(8,128)(2,1)S(1)}, u32[]{:S(2)}, u32[]{:S(2)}) collective-permute-start(bf16[128,2304]{1,0:T(8,128)(2,1)S(1)} %pad_maximum_fusion.1), channel_id=1, source_target_pairs={{0,4},{4,0},{8,12},{12,8},{1,5},{5,1},{9,13},{13,9},{2,6},{6,2},{1... | collective-permute-start | bytes 1769480 | tf_op jit(solution)/shard_map/ppermute | solution.py:21
  4.4 1.5 %collective-permute-start.2 = (bf16[128,2304]{1,0:T(8,128)(2,1)S(1)}, bf16[128,2304]{1,0:T(8,128)(2,1)}, u32[]{:S(2)}, u32[]{:S(2)}) collective-permute-start(bf16[128,2304]{1,0:T(8,128)(2,1)S(1)} %pad_maximum_fusion.1), channel_id=1, source_target_pairs={{4,8},{8,4},{5,9},{9,5},{6,10},{10,6},{7,11},{11,7},{20,24},{24,20... | collective-permute-start | bytes 1769480 | tf_op jit(solution)/shard_map/ppermute | solution.py:138
  5.8 6.1 %fusion.6 = f32[768,1024]{1,0:T(8,128)S(1)} fusion(bf16[768,2048]{1,0:T(8,128)(2,1)} %tokens.3, bf16[2048,1024]{1,0:T(8,128)(2,1)} %param.9), kind=kOutput, calls=%fused_computation.66 | convolution fusion | flops 3221225472 | bytes 10485760 | tf_op jit(solution)/shard_map/dot_general | solution.py:149
  12.0 0.0 copy-start.5
  12.0 0.0 copy-start.6
  12.0 0.1 dynamic-slice_convert_fusion.1
  12.1 0.1 pad_maximum_fusion
  12.2 1.4 %copy-done.3 = f32[768,1024]{1,0:T(8,128)} copy-done((f32[768,1024]{1,0:T(8,128)}, f32[768,1024]{1,0:T(8,128)S(1)}, u32[]{:S(2)}) %copy-start.3) | copy-done | bytes 3145752
  13.7 0.1 select_reduce_fusion
  13.8 0.1 pad_add_fusion.1.numbers
  13.9 0.7 constant_dynamic-update-slice_fusion.4
  14.5 3.1 %collective-permute-done.5.refs_1_ = bf16[128,2304]{1,0:T(8,128)(2,1)S(1)} collective-permute-done((bf16[128,2304]{1,0:T(8,128)(2,1)S(1)}, bf16[128,2304]{1,0:T(8,128)(2,1)S(1)}, u32[]{:S(2)}, u32[]{:S(2)}) %collective-permute-start.5) | collective-permute-done | bytes 589856 | tf_op jit(solution)/shard_map/ppermute | solution.py:21
  17.7 0.7 collective-permute-start.6
  18.4 0.1 pad_add_fusion.numbers
  18.5 1.7 %collective-permute-start.9 = (bf16[128,2304]{1,0:T(8,128)(2,1)S(1)}, bf16[128,2304]{1,0:T(8,128)(2,1)S(1)}, u32[]{:S(2)}, u32[]{:S(2)}) collective-permute-start(bf16[128,2304]{1,0:T(8,128)(2,1)S(1)} %collective-permute-done.5.refs_1_), channel_id=1, source_target_pairs={{0,16},{16,0},{1,17},{17,1},{2,18},{18,2},{3,19},{19,3},{4,20},{20... | collective-permute-start | bytes 1769480 | tf_op jit(solution)/shard_map/ppermute | solution.py:21
  20.3 0.0 collective-permute-done.2
  20.3 1.3 %collective-permute-start.3 = (bf16[128,2304]{1,0:T(8,128)(2,1)}, bf16[128,2304]{1,0:T(8,128)(2,1)S(1)}, u32[]{:S(2)}, u32[]{:S(2)}) collective-permute-start(bf16[128,2304]{1,0:T(8,128)(2,1)} %collective-permute-done.2), channel_id=1, source_target_pairs={{4,0},{8,12},{5,1},{9,13},{6,2},{10,14},{7,3},{11,15},{20,16},{24,... | collective-permute-start | bytes 1769480 | tf_op jit(solution)/shard_map/ppermute | solution.py:135
  21.6 0.6 slice_dynamic-update-slice_fusion.3
  22.2 0.0 collective-permute-done
  22.2 1.4 %add_convert_fusion.1.refs_0_ = bf16[768,256]{1,0:T(8,128)(2,1)S(1)} fusion(f32[768,1024]{1,0:T(8,128)} %copy-done.3, s32[]{:T(128)S(6)} %select_n.129, bf16[768,512]{1,0:T(8,128)(2,1)} %collective-permute-done, s32[]{:T(128)S(6)} %select_n.130), kind=kLoop, calls=%fused_computation.4 | loop fusion | flops 589824 | bytes 1572872 | tf_op jit(solution)/shard_map/convert_element_type | solution.py:161
  23.6 1.6 %collective-permute-start.1 = (bf16[768,256]{1,0:T(8,128)(2,1)S(1)}, bf16[768,256]{1,0:T(8,128)(2,1)S(1)}, u32[]{:S(2)}, u32[]{:S(2)}) collective-permute-start(bf16[768,256]{1,0:T(8,128)(2,1)S(1)} %add_convert_fusion.1.refs_0_), channel_id=1, source_target_pairs={{0,2},{1,3},{2,0},{3,1},{4,6},{5,7},{6,4},{7,5},{8,10},{9,11},{10,... | collective-permute-start | bytes 1179656 | tf_op jit(solution)/shard_map/ppermute | solution.py:21
  25.2 0.5 shard_map.64
  26.4 0.0 copy-start.1
  26.5 1.6 %collective-permute-start.7 = (bf16[64,2304]{1,0:T(8,128)(2,1)S(1)}, bf16[64,2304]{1,0:T(8,128)(2,1)S(1)}, u32[]{:S(2)}, u32[]{:S(2)}) collective-permute-start(bf16[64,2304]{1,0:T(8,128)(2,1)S(1)} %get-tuple-element.7), channel_id=1, source_target_pairs={{4,0},{8,12},{5,1},{9,13},{6,2},{10,14},{7,3},{11,15},{20,16},{24,... | collective-permute-start | bytes 884744 | tf_op jit(solution)/shard_map/ppermute | solution.py:135
  28.0 1.3 %collective-permute-start.8 = (bf16[64,2304]{1,0:T(8,128)(2,1)S(1)}, bf16[64,2304]{1,0:T(8,128)(2,1)S(1)}, u32[]{:S(2)}, u32[]{:S(2)}) collective-permute-start(bf16[64,2304]{1,0:T(8,128)(2,1)S(1)} %get-tuple-element.8), channel_id=1, source_target_pairs={{4,0},{8,12},{5,1},{9,13},{6,2},{10,14},{7,3},{11,15},{20,16},{24,... | collective-permute-start | bytes 884744 | tf_op jit(solution)/shard_map/ppermute | solution.py:135
  29.3 10.6 %collective-permute-done.3 = bf16[128,2304]{1,0:T(8,128)(2,1)S(1)} collective-permute-done((bf16[128,2304]{1,0:T(8,128)(2,1)}, bf16[128,2304]{1,0:T(8,128)(2,1)S(1)}, u32[]{:S(2)}, u32[]{:S(2)}) %collective-permute-start.3) | collective-permute-done | bytes 589856 | tf_op jit(solution)/shard_map/ppermute | solution.py:135
  39.9 0.1 broadcast_select_fusion.refs_0_
  40.0 0.1 collective-permute-start.4
  40.0 0.0 collective-permute-done.9.refs_2_
  40.1 0.5 shard_map.65
  41.2 3.2 %shard_map.66.refs_4_ = f32[64,768]{1,0:T(8,128)S(1)} custom-call(s32[3]{0:T(128)S(1)} %pad_add_fusion.1.numbers, s32[1,768]{1,0:T(1,128)S(1)} %reduce_sum.12.page, bf16[768,2048]{1,0:T(8,128)(2,1)S(1)} %copy-done.1, bf16[256,2048]{1,0:T(8,128)(2,1)S(1)} %bitcast.20, bf16[128,2304]{1,0:T(8,128)(2,1)S(1)} %collective-permute-done.5.refs_1_, ...), custom_call_target="tpu_custom_call" | custom-call | tf_op jit(solution)/shard_map/pallas_call | solution.py:90
  44.4 1.8 %collective-permute-done.7 = bf16[64,2304]{1,0:T(8,128)(2,1)S(1)} collective-permute-done((bf16[64,2304]{1,0:T(8,128)(2,1)S(1)}, bf16[64,2304]{1,0:T(8,128)(2,1)S(1)}, u32[]{:S(2)}, u32[]{:S(2)}) %collective-permute-start.7) | collective-permute-done | bytes 294944 | tf_op jit(solution)/shard_map/ppermute | solution.py:135
  46.2 0.4 collective-permute-start.10
  46.6 4.1 %collective-permute-done.8 = bf16[64,2304]{1,0:T(8,128)(2,1)S(1)} collective-permute-done((bf16[64,2304]{1,0:T(8,128)(2,1)S(1)}, bf16[64,2304]{1,0:T(8,128)(2,1)S(1)}, u32[]{:S(2)}, u32[]{:S(2)}) %collective-permute-start.8) | collective-permute-done | bytes 294944 | tf_op jit(solution)/shard_map/ppermute | solution.py:135
  50.8 0.6 collective-permute-start.11
  51.4 4.9 %collective-permute-done.4.refs_1_ = bf16[128,2304]{1,0:T(8,128)(2,1)S(1)} collective-permute-done((bf16[128,2304]{1,0:T(8,128)(2,1)S(1)}, bf16[128,2304]{1,0:T(8,128)(2,1)S(1)}, u32[]{:S(2)}, u32[]{:S(2)}) %collective-permute-start.4) | collective-permute-done | bytes 589856 | tf_op jit(solution)/shard_map/ppermute | solution.py:21
  56.3 4.8 %shard_map.67 = f32[64,768]{1,0:T(8,128)S(1)} custom-call(s32[4]{0:T(128)S(1)} %pad_add_fusion.numbers, s32[1,768]{1,0:T(1,128)S(1)} %reduce_sum.12.page, bf16[768,2048]{1,0:T(8,128)(2,1)S(1)} %copy-done.1, bf16[128,2304]{1,0:T(8,128)(2,1)S(1)} %broadcast_select_fusion.refs_0_, bf16[128,2304]{1,0:T(8,128)(2,1)S(1)} %collective-permute-done.4.refs_1_, ...), custom_call_target="tpu_custom_call" | custom-call | tf_op jit(solution)/shard_map/pallas_call | solution.py:90
  61.1 1.1 %convolution_select_fusion.1 = f32[64,768]{1,0:T(8,128)S(1)} fusion(bf16[768,2048]{1,0:T(8,128)(2,1)S(1)} %copy-done.1, bf16[64,2304]{1,0:T(8,128)(2,1)S(1)} %collective-permute-done.10, pred[768]{0:T(1024)(128)(4,1)S(1)} %get-tuple-element.29), kind=kOutput, calls=%fused_computation.1 | convolution fusion | flops 201375744 | bytes 3605504 | tf_op jit(solution)/shard_map/dot_general | solution.py:200
  62.2 1.8 %collective-permute-done.11 = bf16[64,2304]{1,0:T(8,128)(2,1)S(1)} collective-permute-done((bf16[64,2304]{1,0:T(8,128)(2,1)S(1)}, bf16[64,2304]{1,0:T(8,128)(2,1)S(1)}, u32[]{:S(2)}, u32[]{:S(2)}) %collective-permute-start.11) | collective-permute-done | bytes 294944 | tf_op jit(solution)/shard_map/ppermute | solution.py:21
  64.0 1.1 %add_convert_fusion.3 = bf16[64,768]{1,0:T(8,128)(2,1)S(1)} fusion(f32[64,768]{1,0:T(8,128)S(1)} %shard_map.67, f32[64,768]{1,0:T(8,128)S(1)} %convolution_select_fusion.1, bf16[768,2048]{1,0:T(8,128)(2,1)S(1)} %copy-done.1, bf16[64,2304]{1,0:T(8,128)(2,1)S(1)} %collective-permute-done.11, pred[768]{0:T(1024)(128)(4,1)S(1)} %get-tuple-element.28), kind=kOutput, calls=%fused_computation.15 | convolution fusion | flops 201523200 | bytes 3900416 | tf_op jit(solution)/shard_map/dot_general | solution.py:200
  65.1 0.1 collective-permute-start.12
  65.2 1.3 %collective-permute-done.12 = bf16[64,768]{1,0:T(8,128)(2,1)S(1)} collective-permute-done((bf16[64,768]{1,0:T(8,128)(2,1)S(1)}, bf16[64,768]{1,0:T(8,128)(2,1)S(1)}, u32[]{:S(2)}, u32[]{:S(2)}) %collective-permute-start.12) | collective-permute-done | bytes 98336 | tf_op jit(solution)/shard_map/ppermute | solution.py:21
  66.5 1.6 %collective-permute-start.13 = (bf16[64,768]{1,0:T(8,128)(2,1)S(1)}, bf16[64,768]{1,0:T(8,128)(2,1)S(1)}, u32[]{:S(2)}, u32[]{:S(2)}) collective-permute-start(bf16[64,768]{1,0:T(8,128)(2,1)S(1)} %fusion.2), channel_id=1, source_target_pairs={{0,2},{1,3},{2,0},{3,1},{4,6},{5,7},{6,4},{7,5},{8,10},{9,11},{10,... | collective-permute-start | bytes 294920 | tf_op jit(solution)/shard_map/ppermute | solution.py:21
  68.0 3.4 %collective-permute-done.13 = bf16[64,768]{1,0:T(8,128)(2,1)S(1)} collective-permute-done((bf16[64,768]{1,0:T(8,128)(2,1)S(1)}, bf16[64,768]{1,0:T(8,128)(2,1)S(1)}, u32[]{:S(2)}, u32[]{:S(2)}) %collective-permute-start.13) | collective-permute-done | bytes 98336 | tf_op jit(solution)/shard_map/ppermute | solution.py:21
  71.4 0.1 select_dynamic-update-slice_fusion.15
  71.9 2.6 %add_convert_fusion = bf16[768,256]{1,0:T(8,128)(2,1)} fusion(bf16[768,256]{1,0:T(8,128)(2,1)S(1)} %collective-permute-done.1.refs_0_, f32[768,1024]{1,0:T(8,128)} %copy-done.3, s32[]{:T(128)S(6)} %select_n.125, bf16[768,512]{1,0:T(8,128)(2,1)} %collective-permute-done, s32[]{:T(128)S(6)} %select_n.128, ...), kind=kOutput, calls=%fused_computation.3 | convolution fusion | flops 403832832 | bytes 4063240 | tf_op jit(solution)/shard_map/dot_general | solution.py:222
  (45 shorter events, 0.7 us)
Async XLA Ops:
  0.0 1.2 %copy-start = (bf16[4,64,1024]{2,1,0:T(8,128)(2,1)S(1)}, bf16[4,64,1024]{2,1,0:T(8,128)(2,1)}, u32[]{:S(2)}) copy-start(bf16[4,64,1024]{2,1,0:T(8,128)(2,1)} %param.11) | copy-start | bytes 1572868
  1.3 16.4 %collective-permute-start.5 = (bf16[128,2304]{1,0:T(8,128)(2,1)S(1)}, bf16[128,2304]{1,0:T(8,128)(2,1)S(1)}, u32[]{:S(2)}, u32[]{:S(2)}) collective-permute-start(bf16[128,2304]{1,0:T(8,128)(2,1)S(1)} %pad_maximum_fusion.1), channel_id=1, source_target_pairs={{0,4},{4,0},{8,12},{12,8},{1,5},{5,1},{9,13},{13,9},{2,6},{6,2},{1... | collective-permute-start | bytes 1769480 | tf_op jit(solution)/shard_map/ppermute | solution.py:21
  4.4 15.9 %collective-permute-start.2 = (bf16[128,2304]{1,0:T(8,128)(2,1)S(1)}, bf16[128,2304]{1,0:T(8,128)(2,1)}, u32[]{:S(2)}, u32[]{:S(2)}) collective-permute-start(bf16[128,2304]{1,0:T(8,128)(2,1)S(1)} %pad_maximum_fusion.1), channel_id=1, source_target_pairs={{4,8},{8,4},{5,9},{9,5},{6,10},{10,6},{7,11},{11,7},{20,24},{24,20... | collective-permute-start | bytes 1769480 | tf_op jit(solution)/shard_map/ppermute | solution.py:138
  12.0 1.6 %copy-start.3 = (f32[768,1024]{1,0:T(8,128)}, f32[768,1024]{1,0:T(8,128)S(1)}, u32[]{:S(2)}) copy-start(f32[768,1024]{1,0:T(8,128)S(1)} %fusion.6) | copy-start | bytes 9437188
  12.0 1.6 %copy-start.5 = (s32[768,1]{0,1:T(1,128)S(1)}, s32[768,1]{0,1:T(1,128)}, u32[]{:S(2)}) copy-start(s32[768,1]{0,1:T(1,128)} %param.7) | copy-start | bytes 9220
  12.0 1.7 %copy-start.6 = (s32[16]{0:T(128)S(1)}, s32[16]{0:T(128)}, u32[]{:S(2)}) copy-start(s32[16]{0:T(128)} %param.8) | copy-start | bytes 196
  13.6 8.6 %collective-permute-start = (bf16[768,512]{1,0:T(8,128)(2,1)S(1)}, bf16[768,512]{1,0:T(8,128)(2,1)}, u32[]{:S(2)}, u32[]{:S(2)}) collective-permute-start(bf16[768,512]{1,0:T(8,128)(2,1)S(1)} %pad_maximum_fusion), channel_id=1, source_target_pairs={{0,1},{1,0},{2,3},{3,2},{4,5},{5,4},{6,7},{7,6},{8,9},{9,8},{10,11... | collective-permute-start | bytes 2359304 | tf_op jit(solution)/shard_map/ppermute | solution.py:21
  17.7 8.7 %collective-permute-start.6 = (bf16[128,2304]{1,0:T(8,128)(2,1)S(1)}, bf16[128,2304]{1,0:T(8,128)(2,1)S(1)}, u32[]{:S(2)}, u32[]{:S(2)}) collective-permute-start(bf16[128,2304]{1,0:T(8,128)(2,1)S(1)} %collective-permute-done.5.refs_1_), channel_id=1, source_target_pairs={{4,8},{8,4},{5,9},{9,5},{6,10},{10,6},{7,11},{11,7},{20,24},{24,20... | collective-permute-start | bytes 1769480 | tf_op jit(solution)/shard_map/ppermute | solution.py:138
  18.5 21.5 %collective-permute-start.9 = (bf16[128,2304]{1,0:T(8,128)(2,1)S(1)}, bf16[128,2304]{1,0:T(8,128)(2,1)S(1)}, u32[]{:S(2)}, u32[]{:S(2)}) collective-permute-start(bf16[128,2304]{1,0:T(8,128)(2,1)S(1)} %collective-permute-done.5.refs_1_), channel_id=1, source_target_pairs={{0,16},{16,0},{1,17},{17,1},{2,18},{18,2},{3,19},{19,3},{4,20},{20... | collective-permute-start | bytes 1769480 | tf_op jit(solution)/shard_map/ppermute | solution.py:21
  20.3 19.6 %collective-permute-start.3 = (bf16[128,2304]{1,0:T(8,128)(2,1)}, bf16[128,2304]{1,0:T(8,128)(2,1)S(1)}, u32[]{:S(2)}, u32[]{:S(2)}) collective-permute-start(bf16[128,2304]{1,0:T(8,128)(2,1)} %collective-permute-done.2), channel_id=1, source_target_pairs={{4,0},{8,12},{5,1},{9,13},{6,2},{10,14},{7,3},{11,15},{20,16},{24,... | collective-permute-start | bytes 1769480 | tf_op jit(solution)/shard_map/ppermute | solution.py:135
  22.2 19.0 %copy-start.2 = (bf16[4,64,2048]{2,1,0:T(8,128)(2,1)S(1)}, bf16[4,64,2048]{2,1,0:T(8,128)(2,1)}, u32[]{:S(2)}) copy-start(bf16[4,64,2048]{2,1,0:T(8,128)(2,1)} %param.10) | copy-start | bytes 3145732
  23.6 16.5 %collective-permute-start.1 = (bf16[768,256]{1,0:T(8,128)(2,1)S(1)}, bf16[768,256]{1,0:T(8,128)(2,1)S(1)}, u32[]{:S(2)}, u32[]{:S(2)}) collective-permute-start(bf16[768,256]{1,0:T(8,128)(2,1)S(1)} %add_convert_fusion.1.refs_0_), channel_id=1, source_target_pairs={{0,2},{1,3},{2,0},{3,1},{4,6},{5,7},{6,4},{7,5},{8,10},{9,11},{10,... | collective-permute-start | bytes 1179656 | tf_op jit(solution)/shard_map/ppermute | solution.py:21
  25.2 14.9 %copy-start.4 = (bf16[1024,256]{1,0:T(8,128)(2,1)S(1)}, bf16[1024,256]{1,0:T(8,128)(2,1)}, u32[]{:S(2)}) copy-start(bf16[1024,256]{1,0:T(8,128)(2,1)} %slice_dynamic-update-slice_fusion.3) | copy-start | bytes 1572868
  26.4 14.8 %copy-start.1 = (bf16[768,2048]{1,0:T(8,128)(2,1)S(1)}, bf16[768,2048]{1,0:T(8,128)(2,1)}, u32[]{:S(2)}) copy-start(bf16[768,2048]{1,0:T(8,128)(2,1)} %tokens.3) | copy-start | bytes 9437188
  26.5 19.7 %collective-permute-start.7 = (bf16[64,2304]{1,0:T(8,128)(2,1)S(1)}, bf16[64,2304]{1,0:T(8,128)(2,1)S(1)}, u32[]{:S(2)}, u32[]{:S(2)}) collective-permute-start(bf16[64,2304]{1,0:T(8,128)(2,1)S(1)} %get-tuple-element.7), channel_id=1, source_target_pairs={{4,0},{8,12},{5,1},{9,13},{6,2},{10,14},{7,3},{11,15},{20,16},{24,... | collective-permute-start | bytes 884744 | tf_op jit(solution)/shard_map/ppermute | solution.py:135
  28.0 22.7 %collective-permute-start.8 = (bf16[64,2304]{1,0:T(8,128)(2,1)S(1)}, bf16[64,2304]{1,0:T(8,128)(2,1)S(1)}, u32[]{:S(2)}, u32[]{:S(2)}) collective-permute-start(bf16[64,2304]{1,0:T(8,128)(2,1)S(1)} %get-tuple-element.8), channel_id=1, source_target_pairs={{4,0},{8,12},{5,1},{9,13},{6,2},{10,14},{7,3},{11,15},{20,16},{24,... | collective-permute-start | bytes 884744 | tf_op jit(solution)/shard_map/ppermute | solution.py:135
  40.0 16.3 %collective-permute-start.4 = (bf16[128,2304]{1,0:T(8,128)(2,1)S(1)}, bf16[128,2304]{1,0:T(8,128)(2,1)S(1)}, u32[]{:S(2)}, u32[]{:S(2)}) collective-permute-start(bf16[128,2304]{1,0:T(8,128)(2,1)S(1)} %broadcast_select_fusion.refs_0_), channel_id=1, source_target_pairs={{0,16},{16,0},{1,17},{17,1},{2,18},{18,2},{3,19},{19,3},{4,20},{20... | collective-permute-start | bytes 1769480 | tf_op jit(solution)/shard_map/ppermute | solution.py:21
  46.2 14.9 %collective-permute-start.10 = (bf16[64,2304]{1,0:T(8,128)(2,1)S(1)}, bf16[64,2304]{1,0:T(8,128)(2,1)S(1)}, u32[]{:S(2)}, u32[]{:S(2)}) collective-permute-start(bf16[64,2304]{1,0:T(8,128)(2,1)S(1)} %broadcast_select_fusion.2.refs_2_), channel_id=1, source_target_pairs={{0,16},{16,0},{1,17},{17,1},{2,18},{18,2},{3,19},{19,3},{4,20},{20... | collective-permute-start | bytes 884744 | tf_op jit(solution)/shard_map/ppermute | solution.py:21
  50.8 13.2 %collective-permute-start.11 = (bf16[64,2304]{1,0:T(8,128)(2,1)S(1)}, bf16[64,2304]{1,0:T(8,128)(2,1)S(1)}, u32[]{:S(2)}, u32[]{:S(2)}) collective-permute-start(bf16[64,2304]{1,0:T(8,128)(2,1)S(1)} %broadcast_select_fusion.1.refs_3_), channel_id=1, source_target_pairs={{0,16},{16,0},{1,17},{17,1},{2,18},{18,2},{3,19},{19,3},{4,20},{20... | collective-permute-start | bytes 884744 | tf_op jit(solution)/shard_map/ppermute | solution.py:21
  65.1 1.4 %collective-permute-start.12 = (bf16[64,768]{1,0:T(8,128)(2,1)S(1)}, bf16[64,768]{1,0:T(8,128)(2,1)S(1)}, u32[]{:S(2)}, u32[]{:S(2)}) collective-permute-start(bf16[64,768]{1,0:T(8,128)(2,1)S(1)} %add_convert_fusion.3), channel_id=1, source_target_pairs={{0,1},{1,0},{2,3},{3,2},{4,5},{5,4},{6,7},{7,6},{8,9},{9,8},{10,11... | collective-permute-start | bytes 294920 | tf_op jit(solution)/shard_map/ppermute | solution.py:21
  66.5 4.9 %collective-permute-start.13 = (bf16[64,768]{1,0:T(8,128)(2,1)S(1)}, bf16[64,768]{1,0:T(8,128)(2,1)S(1)}, u32[]{:S(2)}, u32[]{:S(2)}) collective-permute-start(bf16[64,768]{1,0:T(8,128)(2,1)S(1)} %fusion.2), channel_id=1, source_target_pairs={{0,2},{1,3},{2,0},{3,1},{4,6},{5,7},{6,4},{7,5},{8,10},{9,11},{10,... | collective-permute-start | bytes 294920 | tf_op jit(solution)/shard_map/ppermute | solution.py:21

commit v4 on v3

--- a/solution.py
+++ b/solution.py
@@ -103,6 +103,33 @@
     )(numbers, page, tokens, *weights, *earlier)
 
 
+def last_kernel(total, other_total, page, names, ups, kept, other, out):
+    rank, rows = total.shape
+    tile = 256 if rows % 256 == 0 else rows
+    for t in range(rows // tile):
+        part = slice(t * tile, (t + 1) * tile)
+        shrink = total[:, part] + other_total[:, part].astype(F32)
+        pages = jnp.broadcast_to(page[:, part].astype(F32), (rank, tile))
+        turned = jnp.concatenate([shrink, pages], axis=0).T
+        shrink = turned[:, :rank]
+        wide = jnp.concatenate([shrink] * (ups.shape[0] // rank), axis=1)
+        spread = jnp.where(turned[:, rank : rank + 1] == names[...], wide, 0.0).astype(BF16)
+        delta = jnp.dot(spread, ups[...], preferred_element_type=F32)
+        out[part, :] = (delta + kept[part, :] + other[part, :].astype(F32)).astype(out.dtype)
+
+
+def finish(total, other_total, page, names, ups, kept, other):
+    rows, block = kept.shape
+    return pl.pallas_call(
+        last_kernel,
+        in_specs=[VMEM] * 7,
+        out_specs=VMEM,
+        out_shape=jax.ShapeDtypeStruct((rows, block), BF16),
+        compiler_params=pltpu.CompilerParams(vmem_limit_bytes=12 * MIB),
+        cost_estimate=NO_COST,
+    )(total, other_total, page, names, ups, kept, other)
+
+
 def make(sizes):
     groups, holders, tensor = sizes["groups"], sizes["adapter"], sizes["tensor"]
 
@@ -178,7 +205,6 @@
             halves = lax.optimization_barrier((fmid[:cut], fmid[cut:]))
             lasts = [choose(ready, p, ends(p)) for p in halves]
             ylasts = [across(p) for p in lasts]
-            base = kept + other.astype(F32)
             add(jnp.where(inner == 1, holder ^ 3, holder ^ 2), [far], [yfar])
             add(jnp.where(inner == 1, holder ^ 2, holder ^ 3), lasts, ylasts)
         else:
@@ -204,12 +230,18 @@
         total = shrink.astype(F32)
         if line:
             total = total + swap(shrink, "tensor", tensor, 1).astype(F32)
-            total = total + swap(total.astype(BF16), "tensor", tensor, 2).astype(F32)
+            other_total = swap(total.astype(BF16), "tensor", tensor, 2)
         else:
             for step in range(1, tensor):
                 total = total + shift(shrink, "tensor", tensor, step).astype(F32)
+
+        ups = jnp.concatenate([own_up] + [piece[:, features:] for piece, _ in pieces[1:]], axis=0)
+        if line:
+            names = [first + k for piece, first in pieces for k in range(piece.shape[0] // rank)]
+            names = jnp.repeat(jnp.stack(names).astype(F32), rank)[None, :]
+            return finish(total, other_total, page[None, :], names, ups, kept, other)
+
         total = total.astype(BF16)
-
         spread = jnp.concatenate(
             [
                 jnp.where(page[None, :] == first + k, total, 0)
@@ -218,7 +250,6 @@
             ],
             axis=0,
         )
-        ups = jnp.concatenate([own_up] + [piece[:, features:] for piece, _ in pieces[1:]], axis=0)
         delta = lax.dot_general(spread, ups, (((0,), (0,)), ((), ())), preferred_element_type=F32)
         return (base + delta).astype(BF16)
 

time: 74.8 us -> 71.2 us (0.952)
  waiting for transfers between devices: 30.9 us -> 25.7 us
  starting transfers between devices: 15.4 us -> 18.6 us
  matrix products: 10.9 us -> 8.29 us
  Pallas kernels: 9.09 us -> 10.6 us
    ppermute x9, waiting for transfers between devices: 14.5 us -> 10 us  [swap(): return lax.ppermute(x, axis, [(i, i ^ bit) for i in range(size)])]
    ppermute x9, starting transfers between devices: 9.07 us -> 12.6 us  [swap(): return lax.ppermute(x, axis, [(i, i ^ bit) for i in range(size)])]
    dot_general x1 -> x0, matrix products: 2.62 us -> none  [per_device(): lax.dot_general(spread, ups, (((0,), (0,)), ((), ())), preferred_element_...]
    add x0 -> x1, other arithmetic: none -> 1.74 us  [pick(): return columns(whole, 2 * which + low) + columns(recv, which).astype(F32)]
    pallas_call x0 -> x1, Pallas kernels: none -> 1.51 us  [finish(): pl.pallas_call(last_kernel, in_specs=[VMEM] * 7, out_specs=VMEM, out_shap...]
    convert_element_type x2, other arithmetic: 1.44 us -> 0.03 us  [the longest x1 0.03 us: per_device(): other_total = swap(total.astype(BF16), 'tensor', tensor, 2)]
    unnamed x22 -> x20, local copies, waits for them, and re-layouts: 2.82 us -> 2.17 us
  transfers between devices with their start and end apart: 14 -> 14, of which waited for: 8 -> 8; matrix products, arithmetic and copies ran while one was open for 14% -> 14% of each run, Pallas kernels for 12% -> 13%
where the time goes in v4:
time: 71.2 us; the launch traced here: 70.9 us
  waiting for transfers between devices  25.7 us (36%)
  starting transfers between devices  18.6 us (26%)
  Pallas kernels  10.6 us (15%)
  matrix products  8.29 us (12%)
  local copies, waits for them, and re-layouts  3.73 us (5%)
  other arithmetic  2.26 us (3%)
  between operations  1.62 us (2%)
    ppermute x3, waiting for transfers between devices, ends(): return lax.ppermute(p, 'adapter', [(1, 0), (2, 3)])  15.7 us
    ppermute x9, starting transfers between devices, swap(): return lax.ppermute(x, axis, [(i, i ^ bit) for i in range(size)])  12.6 us
    ppermute x9, waiting for transfers between devices, swap(): return lax.ppermute(x, axis, [(i, i ^ bit) for i in range(size)])  10 us
    pallas_call x2, Pallas kernels, shrink_many(): pl.pallas_call(functools.partial(many_kernel, rank, len(weights)), in_spe...  8.04 us
    dot_general x1, matrix products, per_device(): whole = jnp.dot(tokens, base_weight, preferred_element_type=F32)  6.13 us
    ppermute x3, starting transfers between devices, ends(): return lax.ppermute(p, 'adapter', [(1, 0), (2, 3)])  3.88 us
    ppermute x2, starting transfers between devices, middle(): return lax.ppermute(p, 'adapter', [(1, 2), (2, 1)])  2.17 us
    unnamed x20, local copies, waits for them, and re-layouts  2.17 us
  transfers between devices with their start and end apart: 14, of which 8 were waited for; matrix products, arithmetic and copies ran while one was open for 14% of the time, Pallas kernels for 13%

profile of v4, /device:TPU:0, one launch (start us, length us, event | category | flops | bytes accessed | tf_op | source)
XLA Modules:
  0.0 70.9 jit_solution(10371823248476458733)
XLA Ops:
  0.0 1.1 %constant_dynamic-slice_fusion.2 = bf16[2,64,2048]{2,1,0:T(8,128)(2,1)S(1)} fusion(bf16[4,64,2048]{2,1,0:T(8,128)(2,1)} %param.10, s32[]{:T(128)S(6)} %select_n.84), kind=kLoop, calls=%fused_computation.28 | loop fusion | bytes 1048580 | tf_op jit(solution)/shard_map/dynamic_slice | solution.py:151
  1.1 0.1 copy-done
  1.3 1.5 %collective-permute-start.1 = (bf16[128,2304]{1,0:T(8,128)(2,1)S(1)}, bf16[128,2304]{1,0:T(8,128)(2,1)}, u32[]{:S(2)}, u32[]{:S(2)}) collective-permute-start(bf16[128,2304]{1,0:T(8,128)(2,1)S(1)} %pad_maximum_fusion.1), channel_id=1, source_target_pairs={{4,8},{8,4},{5,9},{9,5},{6,10},{10,6},{7,11},{11,7},{20,24},{24,20... | collective-permute-start | bytes 1769480 | tf_op jit(solution)/shard_map/ppermute | solution.py:165
  2.7 5.1 %collective-permute-start.5 = (bf16[128,2304]{1,0:T(8,128)(2,1)S(1)}, bf16[128,2304]{1,0:T(8,128)(2,1)S(1)}, u32[]{:S(2)}, u32[]{:S(2)}) collective-permute-start(bf16[128,2304]{1,0:T(8,128)(2,1)S(1)} %pad_maximum_fusion.1), channel_id=1, source_target_pairs={{0,4},{4,0},{8,12},{12,8},{1,5},{5,1},{9,13},{13,9},{2,6},{6,2},{1... | collective-permute-start | bytes 1769480 | tf_op jit(solution)/shard_map/ppermute | solution.py:21
  7.8 6.1 %fusion.6 = f32[768,1024]{1,0:T(8,128)S(1)} fusion(bf16[768,2048]{1,0:T(8,128)(2,1)} %tokens.3, bf16[2048,1024]{1,0:T(8,128)(2,1)} %param.9), kind=kOutput, calls=%fused_computation.35 | convolution fusion | flops 3221225472 | bytes 10485760 | tf_op jit(solution)/shard_map/dot_general | solution.py:176
  14.0 1.6 %copy-done.3 = f32[768,1024]{1,0:T(8,128)} copy-done((f32[768,1024]{1,0:T(8,128)}, f32[768,1024]{1,0:T(8,128)S(1)}, u32[]{:S(2)}) %copy-start.3) | copy-done | bytes 3145752
  15.6 0.1 dynamic-slice_convert_fusion.1
  15.7 0.1 pad_maximum_fusion
  15.8 0.1 collective-permute-start
  15.9 0.4 copy-done.4
  16.3 0.1 select_reduce_fusion
  16.4 0.1 pad_add_fusion.1.numbers
  16.5 0.1 stack.82
  16.6 0.1 broadcast_in_dim.48
  16.7 0.1 broadcast_in_dim_reshape.3.names
  16.8 0.1 pad_add_fusion.numbers
  16.9 1.3 %collective-permute-start.2 = (bf16[128,2304]{1,0:T(8,128)(2,1)}, bf16[128,2304]{1,0:T(8,128)(2,1)S(1)}, u32[]{:S(2)}, u32[]{:S(2)}) collective-permute-start(bf16[128,2304]{1,0:T(8,128)(2,1)} %collective-permute-done.1), channel_id=1, source_target_pairs={{4,0},{8,12},{5,1},{9,13},{6,2},{10,14},{7,3},{11,15},{20,16},{24,... | collective-permute-start | bytes 1769480 | tf_op jit(solution)/shard_map/ppermute | solution.py:162
  18.2 2.6 %collective-permute-done.5.refs_1_ = bf16[128,2304]{1,0:T(8,128)(2,1)S(1)} collective-permute-done((bf16[128,2304]{1,0:T(8,128)(2,1)S(1)}, bf16[128,2304]{1,0:T(8,128)(2,1)S(1)}, u32[]{:S(2)}, u32[]{:S(2)}) %collective-permute-start.5) | collective-permute-done | bytes 589856 | tf_op jit(solution)/shard_map/ppermute | solution.py:21
  20.9 1.5 %collective-permute-start.9 = (bf16[128,2304]{1,0:T(8,128)(2,1)S(1)}, bf16[128,2304]{1,0:T(8,128)(2,1)S(1)}, u32[]{:S(2)}, u32[]{:S(2)}) collective-permute-start(bf16[128,2304]{1,0:T(8,128)(2,1)S(1)} %collective-permute-done.5.refs_1_), channel_id=1, source_target_pairs={{0,16},{16,0},{1,17},{17,1},{2,18},{18,2},{3,19},{19,3},{4,20},{20... | collective-permute-start | bytes 1769480 | tf_op jit(solution)/shard_map/ppermute | solution.py:21
  22.4 0.7 collective-permute-start.6
  23.1 0.0 copy-start.1
  23.1 0.0 copy-start.2
  23.1 0.0 collective-permute-done
  23.2 1.7 %convert_add_fusion = (f32[768,256]{1,0:T(8,128)S(1)}, bf16[768,256]{1,0:T(8,128)(2,1)S(1)}) fusion(f32[768,1024]{1,0:T(8,128)} %copy-done.3, s32[]{:T(128)S(6)} %select_n.92, bf16[768,512]{1,0:T(8,128)(2,1)S(1)} %collective-permute-done, s32[]{:T(128)S(6)} %select_n.93, s32[]{:T(128)S(6)} %select_n.82, s32[]{:T(128)S(6)} %select_n.79), kind=kLoop, calls=%fused_computation.3 | loop fusion | flops 983040 | bytes 3538960 | tf_op jit(solution)/shard_map/add | solution.py:186
  24.9 1.6 %collective-permute-start.4 = (bf16[768,256]{1,0:T(8,128)(2,1)S(1)}, bf16[768,256]{1,0:T(8,128)(2,1)S(1)}, u32[]{:S(2)}, u32[]{:S(2)}) collective-permute-start(bf16[768,256]{1,0:T(8,128)(2,1)S(1)} %get-tuple-element.10.refs_0_), channel_id=1, source_target_pairs={{0,2},{1,3},{2,0},{3,1},{4,6},{5,7},{6,4},{7,5},{8,10},{9,11},{10,... | collective-permute-start | bytes 1179656 | tf_op jit(solution)/shard_map/ppermute | solution.py:21
  26.5 0.5 shard_map.64
  27.5 7.7 %collective-permute-done.2 = bf16[128,2304]{1,0:T(8,128)(2,1)S(1)} collective-permute-done((bf16[128,2304]{1,0:T(8,128)(2,1)}, bf16[128,2304]{1,0:T(8,128)(2,1)S(1)}, u32[]{:S(2)}, u32[]{:S(2)}) %collective-permute-start.2) | collective-permute-done | bytes 589856 | tf_op jit(solution)/shard_map/ppermute | solution.py:162
  35.3 0.1 broadcast_select_fusion.refs_0_
  35.4 1.6 %collective-permute-start.3 = (bf16[128,2304]{1,0:T(8,128)(2,1)S(1)}, bf16[128,2304]{1,0:T(8,128)(2,1)S(1)}, u32[]{:S(2)}, u32[]{:S(2)}) collective-permute-start(bf16[128,2304]{1,0:T(8,128)(2,1)S(1)} %broadcast_select_fusion.refs_0_), channel_id=1, source_target_pairs={{0,16},{16,0},{1,17},{17,1},{2,18},{18,2},{3,19},{19,3},{4,20},{20... | collective-permute-start | bytes 1769480 | tf_op jit(solution)/shard_map/ppermute | solution.py:21
  37.0 1.3 %collective-permute-start.7 = (bf16[64,2304]{1,0:T(8,128)(2,1)S(1)}, bf16[64,2304]{1,0:T(8,128)(2,1)S(1)}, u32[]{:S(2)}, u32[]{:S(2)}) collective-permute-start(bf16[64,2304]{1,0:T(8,128)(2,1)S(1)} %get-tuple-element.7), channel_id=1, source_target_pairs={{4,0},{8,12},{5,1},{9,13},{6,2},{10,14},{7,3},{11,15},{20,16},{24,... | collective-permute-start | bytes 884744 | tf_op jit(solution)/shard_map/ppermute | solution.py:162
  38.3 1.3 %collective-permute-start.8 = (bf16[64,2304]{1,0:T(8,128)(2,1)S(1)}, bf16[64,2304]{1,0:T(8,128)(2,1)S(1)}, u32[]{:S(2)}, u32[]{:S(2)}) collective-permute-start(bf16[64,2304]{1,0:T(8,128)(2,1)S(1)} %get-tuple-element.8), channel_id=1, source_target_pairs={{4,0},{8,12},{5,1},{9,13},{6,2},{10,14},{7,3},{11,15},{20,16},{24,... | collective-permute-start | bytes 884744 | tf_op jit(solution)/shard_map/ppermute | solution.py:162
  39.6 0.0 collective-permute-done.9.refs_2_
  39.6 0.5 shard_map.65
  40.9 3.2 %shard_map.66.refs_4_ = f32[64,768]{1,0:T(8,128)S(1)} custom-call(s32[3]{0:T(128)S(1)} %pad_add_fusion.1.numbers, s32[1,768]{1,0:T(1,128)S(1)} %broadcast_in_dim.44.page, bf16[768,2048]{1,0:T(8,128)(2,1)S(1)} %copy-done.1, bf16[256,2048]{1,0:T(8,128)(2,1)S(1)} %bitcast.27, bf16[128,2304]{1,0:T(8,128)(2,1)S(1)} %collective-permute-done.5.refs_1_, ...), custom_call_target="tpu_custom_call" | custom-call | tf_op jit(solution)/shard_map/pallas_call | solution.py:90
  44.1 5.2 %collective-permute-done.7 = bf16[64,2304]{1,0:T(8,128)(2,1)S(1)} collective-permute-done((bf16[64,2304]{1,0:T(8,128)(2,1)S(1)}, bf16[64,2304]{1,0:T(8,128)(2,1)S(1)}, u32[]{:S(2)}, u32[]{:S(2)}) %collective-permute-start.7) | collective-permute-done | bytes 294944 | tf_op jit(solution)/shard_map/ppermute | solution.py:162
  49.4 0.6 collective-permute-start.10
  49.9 2.7 %collective-permute-done.8 = bf16[64,2304]{1,0:T(8,128)(2,1)S(1)} collective-permute-done((bf16[64,2304]{1,0:T(8,128)(2,1)S(1)}, bf16[64,2304]{1,0:T(8,128)(2,1)S(1)}, u32[]{:S(2)}, u32[]{:S(2)}) %collective-permute-start.8) | collective-permute-done | bytes 294944 | tf_op jit(solution)/shard_map/ppermute | solution.py:162
  52.7 0.6 collective-permute-start.11
  53.3 4.8 %shard_map.67 = f32[64,768]{1,0:T(8,128)S(1)} custom-call(s32[4]{0:T(128)S(1)} %pad_add_fusion.numbers, s32[1,768]{1,0:T(1,128)S(1)} %broadcast_in_dim.44.page, bf16[768,2048]{1,0:T(8,128)(2,1)S(1)} %copy-done.1, bf16[128,2304]{1,0:T(8,128)(2,1)S(1)} %broadcast_select_fusion.refs_0_, bf16[128,2304]{1,0:T(8,128)(2,1)S(1)} %collective-permute-done.3.refs_1_, ...), custom_call_target="tpu_custom_call" | custom-call | tf_op jit(solution)/shard_map/pallas_call | solution.py:90
  58.1 0.7 collective-permute-done.10
  58.8 1.1 %convolution_select_fusion.1 = f32[64,768]{1,0:T(8,128)S(1)} fusion(bf16[768,2048]{1,0:T(8,128)(2,1)S(1)} %copy-done.1, bf16[64,2304]{1,0:T(8,128)(2,1)S(1)} %collective-permute-done.10, pred[768]{0:T(1024)(128)(4,1)S(1)} %get-tuple-element.18), kind=kOutput, calls=%fused_computation.1 | convolution fusion | flops 201375744 | bytes 3605504 | tf_op jit(solution)/shard_map/dot_general | solution.py:226
  59.9 2.1 %collective-permute-done.11 = bf16[64,2304]{1,0:T(8,128)(2,1)S(1)} collective-permute-done((bf16[64,2304]{1,0:T(8,128)(2,1)S(1)}, bf16[64,2304]{1,0:T(8,128)(2,1)S(1)}, u32[]{:S(2)}, u32[]{:S(2)}) %collective-permute-start.11) | collective-permute-done | bytes 294944 | tf_op jit(solution)/shard_map/ppermute | solution.py:21
  62.0 1.1 %add_convert_fusion.1 = bf16[64,768]{1,0:T(8,128)(2,1)S(1)} fusion(f32[64,768]{1,0:T(8,128)S(1)} %shard_map.67, f32[64,768]{1,0:T(8,128)S(1)} %convolution_select_fusion.1, bf16[768,2048]{1,0:T(8,128)(2,1)S(1)} %copy-done.1, bf16[64,2304]{1,0:T(8,128)(2,1)S(1)} %collective-permute-done.11, pred[768]{0:T(1024)(128)(4,1)S(1)} %get-tuple-element.17), kind=kOutput, calls=%fused_computation.14 | convolution fusion | flops 201523200 | bytes 3900416 | tf_op jit(solution)/shard_map/dot_general | solution.py:226
  63.0 0.1 collective-permute-start.12
  63.1 1.3 %collective-permute-done.12 = bf16[64,768]{1,0:T(8,128)(2,1)S(1)} collective-permute-done((bf16[64,768]{1,0:T(8,128)(2,1)S(1)}, bf16[64,768]{1,0:T(8,128)(2,1)S(1)}, u32[]{:S(2)}, u32[]{:S(2)}) %collective-permute-start.12) | collective-permute-done | bytes 98336 | tf_op jit(solution)/shard_map/ppermute | solution.py:21
  64.4 1.6 %collective-permute-start.13 = (bf16[64,768]{1,0:T(8,128)(2,1)S(1)}, bf16[64,768]{1,0:T(8,128)(2,1)S(1)}, u32[]{:S(2)}, u32[]{:S(2)}) collective-permute-start(bf16[64,768]{1,0:T(8,128)(2,1)S(1)} %get-tuple-element.15), channel_id=1, source_target_pairs={{0,2},{1,3},{2,0},{3,1},{4,6},{5,7},{6,4},{7,5},{8,10},{9,11},{10,... | collective-permute-start | bytes 294920 | tf_op jit(solution)/shard_map/ppermute | solution.py:21
  66.0 3.4 %collective-permute-done.13.other_total = bf16[64,768]{1,0:T(8,128)(2,1)S(1)} collective-permute-done((bf16[64,768]{1,0:T(8,128)(2,1)S(1)}, bf16[64,768]{1,0:T(8,128)(2,1)S(1)}, u32[]{:S(2)}, u32[]{:S(2)}) %collective-permute-start.13) | collective-permute-done | bytes 98336 | tf_op jit(solution)/shard_map/ppermute | solution.py:21
  69.4 1.5 %shard_map.68 = bf16[768,256]{1,0:T(8,128)(2,1)} custom-call(f32[64,768]{1,0:T(8,128)S(1)} %get-tuple-element.16.total, bf16[64,768]{1,0:T(8,128)(2,1)S(1)} %collective-permute-done.13.other_total, s32[1,768]{1,0:T(1,128)S(1)} %broadcast_in_dim.44.page, f32[1,1024]{1,0:T(1,128)S(1)} %broadcast_in_dim_reshape.3.names, ...), custom_call_target="tpu_custom_call" | custom-call | tf_op jit(solution)/shard_map/pallas_call | solution.py:123
  (31 shorter events, 0.3 us)
Async XLA Ops:
  0.0 1.2 %copy-start = (bf16[4,64,1024]{2,1,0:T(8,128)(2,1)S(1)}, bf16[4,64,1024]{2,1,0:T(8,128)(2,1)}, u32[]{:S(2)}) copy-start(bf16[4,64,1024]{2,1,0:T(8,128)(2,1)} %param.11) | copy-start | bytes 1572868
  1.3 15.7 %collective-permute-start.1 = (bf16[128,2304]{1,0:T(8,128)(2,1)S(1)}, bf16[128,2304]{1,0:T(8,128)(2,1)}, u32[]{:S(2)}, u32[]{:S(2)}) collective-permute-start(bf16[128,2304]{1,0:T(8,128)(2,1)S(1)} %pad_maximum_fusion.1), channel_id=1, source_target_pairs={{4,8},{8,4},{5,9},{9,5},{6,10},{10,6},{7,11},{11,7},{20,24},{24,20... | collective-permute-start | bytes 1769480 | tf_op jit(solution)/shard_map/ppermute | solution.py:165
  2.7 18.1 %collective-permute-start.5 = (bf16[128,2304]{1,0:T(8,128)(2,1)S(1)}, bf16[128,2304]{1,0:T(8,128)(2,1)S(1)}, u32[]{:S(2)}, u32[]{:S(2)}) collective-permute-start(bf16[128,2304]{1,0:T(8,128)(2,1)S(1)} %pad_maximum_fusion.1), channel_id=1, source_target_pairs={{0,4},{4,0},{8,12},{12,8},{1,5},{5,1},{9,13},{13,9},{2,6},{6,2},{1... | collective-permute-start | bytes 1769480 | tf_op jit(solution)/shard_map/ppermute | solution.py:21
  14.0 1.6 %copy-start.3 = (f32[768,1024]{1,0:T(8,128)}, f32[768,1024]{1,0:T(8,128)S(1)}, u32[]{:S(2)}) copy-start(f32[768,1024]{1,0:T(8,128)S(1)} %fusion.6) | copy-start | bytes 9437188
  15.6 0.7 copy-start.4
  15.6 0.7 copy-start.5
  15.8 7.3 %collective-permute-start = (bf16[768,512]{1,0:T(8,128)(2,1)S(1)}, bf16[768,512]{1,0:T(8,128)(2,1)S(1)}, u32[]{:S(2)}, u32[]{:S(2)}) collective-permute-start(bf16[768,512]{1,0:T(8,128)(2,1)S(1)} %pad_maximum_fusion), channel_id=1, source_target_pairs={{0,1},{1,0},{2,3},{3,2},{4,5},{5,4},{6,7},{7,6},{8,9},{9,8},{10,11... | collective-permute-start | bytes 2359304 | tf_op jit(solution)/shard_map/ppermute | solution.py:21
  16.9 18.4 %collective-permute-start.2 = (bf16[128,2304]{1,0:T(8,128)(2,1)}, bf16[128,2304]{1,0:T(8,128)(2,1)S(1)}, u32[]{:S(2)}, u32[]{:S(2)}) collective-permute-start(bf16[128,2304]{1,0:T(8,128)(2,1)} %collective-permute-done.1), channel_id=1, source_target_pairs={{4,0},{8,12},{5,1},{9,13},{6,2},{10,14},{7,3},{11,15},{20,16},{24,... | collective-permute-start | bytes 1769480 | tf_op jit(solution)/shard_map/ppermute | solution.py:162
  20.9 18.7 %collective-permute-start.9 = (bf16[128,2304]{1,0:T(8,128)(2,1)S(1)}, bf16[128,2304]{1,0:T(8,128)(2,1)S(1)}, u32[]{:S(2)}, u32[]{:S(2)}) collective-permute-start(bf16[128,2304]{1,0:T(8,128)(2,1)S(1)} %collective-permute-done.5.refs_1_), channel_id=1, source_target_pairs={{0,16},{16,0},{1,17},{17,1},{2,18},{18,2},{3,19},{19,3},{4,20},{20... | collective-permute-start | bytes 1769480 | tf_op jit(solution)/shard_map/ppermute | solution.py:21
  22.4 14.5 %collective-permute-start.6 = (bf16[128,2304]{1,0:T(8,128)(2,1)S(1)}, bf16[128,2304]{1,0:T(8,128)(2,1)S(1)}, u32[]{:S(2)}, u32[]{:S(2)}) collective-permute-start(bf16[128,2304]{1,0:T(8,128)(2,1)S(1)} %collective-permute-done.5.refs_1_), channel_id=1, source_target_pairs={{4,8},{8,4},{5,9},{9,5},{6,10},{10,6},{7,11},{11,7},{20,24},{24,20... | collective-permute-start | bytes 1769480 | tf_op jit(solution)/shard_map/ppermute | solution.py:165
  23.1 17.7 %copy-start.1 = (bf16[768,2048]{1,0:T(8,128)(2,1)S(1)}, bf16[768,2048]{1,0:T(8,128)(2,1)}, u32[]{:S(2)}) copy-start(bf16[768,2048]{1,0:T(8,128)(2,1)} %tokens.3) | copy-start | bytes 9437188
  23.1 17.7 %copy-start.2 = (bf16[4,64,2048]{2,1,0:T(8,128)(2,1)S(1)}, bf16[4,64,2048]{2,1,0:T(8,128)(2,1)}, u32[]{:S(2)}) copy-start(bf16[4,64,2048]{2,1,0:T(8,128)(2,1)} %param.10) | copy-start | bytes 3145732
  24.9 14.7 %collective-permute-start.4 = (bf16[768,256]{1,0:T(8,128)(2,1)S(1)}, bf16[768,256]{1,0:T(8,128)(2,1)S(1)}, u32[]{:S(2)}, u32[]{:S(2)}) collective-permute-start(bf16[768,256]{1,0:T(8,128)(2,1)S(1)} %get-tuple-element.10.refs_0_), channel_id=1, source_target_pairs={{0,2},{1,3},{2,0},{3,1},{4,6},{5,7},{6,4},{7,5},{8,10},{9,11},{10,... | collective-permute-start | bytes 1179656 | tf_op jit(solution)/shard_map/ppermute | solution.py:21
  35.4 17.9 %collective-permute-start.3 = (bf16[128,2304]{1,0:T(8,128)(2,1)S(1)}, bf16[128,2304]{1,0:T(8,128)(2,1)S(1)}, u32[]{:S(2)}, u32[]{:S(2)}) collective-permute-start(bf16[128,2304]{1,0:T(8,128)(2,1)S(1)} %broadcast_select_fusion.refs_0_), channel_id=1, source_target_pairs={{0,16},{16,0},{1,17},{17,1},{2,18},{18,2},{3,19},{19,3},{4,20},{20... | collective-permute-start | bytes 1769480 | tf_op jit(solution)/shard_map/ppermute | solution.py:21
  37.0 12.3 %collective-permute-start.7 = (bf16[64,2304]{1,0:T(8,128)(2,1)S(1)}, bf16[64,2304]{1,0:T(8,128)(2,1)S(1)}, u32[]{:S(2)}, u32[]{:S(2)}) collective-permute-start(bf16[64,2304]{1,0:T(8,128)(2,1)S(1)} %get-tuple-element.7), channel_id=1, source_target_pairs={{4,0},{8,12},{5,1},{9,13},{6,2},{10,14},{7,3},{11,15},{20,16},{24,... | collective-permute-start | bytes 884744 | tf_op jit(solution)/shard_map/ppermute | solution.py:162
  38.3 14.4 %collective-permute-start.8 = (bf16[64,2304]{1,0:T(8,128)(2,1)S(1)}, bf16[64,2304]{1,0:T(8,128)(2,1)S(1)}, u32[]{:S(2)}, u32[]{:S(2)}) collective-permute-start(bf16[64,2304]{1,0:T(8,128)(2,1)S(1)} %get-tuple-element.8), channel_id=1, source_target_pairs={{4,0},{8,12},{5,1},{9,13},{6,2},{10,14},{7,3},{11,15},{20,16},{24,... | collective-permute-start | bytes 884744 | tf_op jit(solution)/shard_map/ppermute | solution.py:162
  49.4 9.4 %collective-permute-start.10 = (bf16[64,2304]{1,0:T(8,128)(2,1)S(1)}, bf16[64,2304]{1,0:T(8,128)(2,1)S(1)}, u32[]{:S(2)}, u32[]{:S(2)}) collective-permute-start(bf16[64,2304]{1,0:T(8,128)(2,1)S(1)} %broadcast_select_fusion.2.refs_2_), channel_id=1, source_target_pairs={{0,16},{16,0},{1,17},{17,1},{2,18},{18,2},{3,19},{19,3},{4,20},{20... | collective-permute-start | bytes 884744 | tf_op jit(solution)/shard_map/ppermute | solution.py:21
  52.7 9.3 %collective-permute-start.11 = (bf16[64,2304]{1,0:T(8,128)(2,1)S(1)}, bf16[64,2304]{1,0:T(8,128)(2,1)S(1)}, u32[]{:S(2)}, u32[]{:S(2)}) collective-permute-start(bf16[64,2304]{1,0:T(8,128)(2,1)S(1)} %broadcast_select_fusion.1.refs_3_), channel_id=1, source_target_pairs={{0,16},{16,0},{1,17},{17,1},{2,18},{18,2},{3,19},{19,3},{4,20},{20... | collective-permute-start | bytes 884744 | tf_op jit(solution)/shard_map/ppermute | solution.py:21
  63.0 1.4 %collective-permute-start.12 = (bf16[64,768]{1,0:T(8,128)(2,1)S(1)}, bf16[64,768]{1,0:T(8,128)(2,1)S(1)}, u32[]{:S(2)}, u32[]{:S(2)}) collective-permute-start(bf16[64,768]{1,0:T(8,128)(2,1)S(1)} %add_convert_fusion.1), channel_id=1, source_target_pairs={{0,1},{1,0},{2,3},{3,2},{4,5},{5,4},{6,7},{7,6},{8,9},{9,8},{10,11... | collective-permute-start | bytes 294920 | tf_op jit(solution)/shard_map/ppermute | solution.py:21
  64.4 4.9 %collective-permute-start.13 = (bf16[64,768]{1,0:T(8,128)(2,1)S(1)}, bf16[64,768]{1,0:T(8,128)(2,1)S(1)}, u32[]{:S(2)}, u32[]{:S(2)}) collective-permute-start(bf16[64,768]{1,0:T(8,128)(2,1)S(1)} %get-tuple-element.15), channel_id=1, source_target_pairs={{0,2},{1,3},{2,0},{3,1},{4,6},{5,7},{6,4},{7,5},{8,10},{9,11},{10,... | collective-permute-start | bytes 294920 | tf_op jit(solution)/shard_map/ppermute | solution.py:21

commit v5 on v4

--- a/solution.py
+++ b/solution.py
@@ -229,8 +229,8 @@
         shrink = shrink.astype(BF16)
         total = shrink.astype(F32)
         if line:
-            total = total + swap(shrink, "tensor", tensor, 1).astype(F32)
-            other_total = swap(total.astype(BF16), "tensor", tensor, 2)
+            total = total + swap(shrink, "tensor", tensor, 2).astype(F32)
+            other_total = swap(total, "tensor", tensor, 1)
         else:
             for step in range(1, tensor):
                 total = total + shift(shrink, "tensor", tensor, step).astype(F32)

time: 71.2 us -> 71.1 us (level)
  no operation moved by 1% of the time
where the time goes in v5:
time: 71.1 us; the launch traced here: 70.8 us
  waiting for transfers between devices  25.5 us (36%)
  starting transfers between devices  18.6 us (26%)
  Pallas kernels  10.6 us (15%)
  matrix products  8.29 us (12%)
  local copies, waits for them, and re-layouts  3.74 us (5%)
  other arithmetic  2.26 us (3%)
  between operations  1.74 us (2%)
    ppermute x3, waiting for transfers between devices, ends(): return lax.ppermute(p, 'adapter', [(1, 0), (2, 3)])  15.5 us
    ppermute x9, starting transfers between devices, swap(): return lax.ppermute(x, axis, [(i, i ^ bit) for i in range(size)])  12.6 us
    ppermute x9, waiting for transfers between devices, swap(): return lax.ppermute(x, axis, [(i, i ^ bit) for i in range(size)])  9.95 us
    pallas_call x2, Pallas kernels, shrink_many(): pl.pallas_call(functools.partial(many_kernel, rank, len(weights)), in_spe...  8.05 us
    dot_general x1, matrix products, per_device(): whole = jnp.dot(tokens, base_weight, preferred_element_type=F32)  6.13 us
    ppermute x3, starting transfers between devices, ends(): return lax.ppermute(p, 'adapter', [(1, 0), (2, 3)])  3.88 us
    ppermute x2, starting transfers between devices, middle(): return lax.ppermute(p, 'adapter', [(1, 2), (2, 1)])  2.17 us
    unnamed x20, local copies, waits for them, and re-layouts  2.17 us
  transfers between devices with their start and end apart: 14, of which 8 were waited for; matrix products, arithmetic and copies ran while one was open for 14% of the time, Pallas kernels for 13%

profile of v5, /device:TPU:0, one launch (start us, length us, event | category | flops | bytes accessed | tf_op | source)
XLA Modules:
  0.0 70.8 jit_solution(14619989357484912123)
XLA Ops:
  0.0 1.1 %constant_dynamic-slice_fusion.2 = bf16[2,64,2048]{2,1,0:T(8,128)(2,1)S(1)} fusion(bf16[4,64,2048]{2,1,0:T(8,128)(2,1)} %param.10, s32[]{:T(128)S(6)} %select_n.84), kind=kLoop, calls=%fused_computation.28 | loop fusion | bytes 1048580 | tf_op jit(solution)/shard_map/dynamic_slice | solution.py:151
  1.1 0.1 copy-done
  1.3 1.5 %collective-permute-start.1 = (bf16[128,2304]{1,0:T(8,128)(2,1)S(1)}, bf16[128,2304]{1,0:T(8,128)(2,1)}, u32[]{:S(2)}, u32[]{:S(2)}) collective-permute-start(bf16[128,2304]{1,0:T(8,128)(2,1)S(1)} %pad_maximum_fusion.1), channel_id=1, source_target_pairs={{4,8},{8,4},{5,9},{9,5},{6,10},{10,6},{7,11},{11,7},{20,24},{24,20... | collective-permute-start | bytes 1769480 | tf_op jit(solution)/shard_map/ppermute | solution.py:165
  2.7 5.1 %collective-permute-start.5 = (bf16[128,2304]{1,0:T(8,128)(2,1)S(1)}, bf16[128,2304]{1,0:T(8,128)(2,1)S(1)}, u32[]{:S(2)}, u32[]{:S(2)}) collective-permute-start(bf16[128,2304]{1,0:T(8,128)(2,1)S(1)} %pad_maximum_fusion.1), channel_id=1, source_target_pairs={{0,4},{4,0},{8,12},{12,8},{1,5},{5,1},{9,13},{13,9},{2,6},{6,2},{1... | collective-permute-start | bytes 1769480 | tf_op jit(solution)/shard_map/ppermute | solution.py:21
  7.8 6.1 %fusion.5 = f32[768,1024]{1,0:T(8,128)S(1)} fusion(bf16[768,2048]{1,0:T(8,128)(2,1)} %tokens.3, bf16[2048,1024]{1,0:T(8,128)(2,1)} %param.9), kind=kOutput, calls=%fused_computation.34 | convolution fusion | flops 3221225472 | bytes 10485760 | tf_op jit(solution)/shard_map/dot_general | solution.py:176
  14.0 1.6 %copy-done.3 = f32[768,1024]{1,0:T(8,128)} copy-done((f32[768,1024]{1,0:T(8,128)}, f32[768,1024]{1,0:T(8,128)S(1)}, u32[]{:S(2)}) %copy-start.3) | copy-done | bytes 3145752
  15.6 0.1 dynamic-slice_convert_fusion.1
  15.7 0.1 pad_maximum_fusion
  15.8 0.1 collective-permute-start
  15.9 0.4 copy-done.4
  16.3 0.1 select_reduce_fusion
  16.4 0.1 pad_add_fusion.1.numbers
  16.5 0.1 stack.82
  16.6 0.1 broadcast_in_dim.48
  16.7 0.1 broadcast_in_dim_reshape.3.names
  16.8 0.1 pad_add_fusion.numbers
  16.9 1.3 %collective-permute-start.2 = (bf16[128,2304]{1,0:T(8,128)(2,1)}, bf16[128,2304]{1,0:T(8,128)(2,1)S(1)}, u32[]{:S(2)}, u32[]{:S(2)}) collective-permute-start(bf16[128,2304]{1,0:T(8,128)(2,1)} %collective-permute-done.1), channel_id=1, source_target_pairs={{4,0},{8,12},{5,1},{9,13},{6,2},{10,14},{7,3},{11,15},{20,16},{24,... | collective-permute-start | bytes 1769480 | tf_op jit(solution)/shard_map/ppermute | solution.py:162
  18.3 2.6 %collective-permute-done.5.refs_1_ = bf16[128,2304]{1,0:T(8,128)(2,1)S(1)} collective-permute-done((bf16[128,2304]{1,0:T(8,128)(2,1)S(1)}, bf16[128,2304]{1,0:T(8,128)(2,1)S(1)}, u32[]{:S(2)}, u32[]{:S(2)}) %collective-permute-start.5) | collective-permute-done | bytes 589856 | tf_op jit(solution)/shard_map/ppermute | solution.py:21
  20.9 1.5 %collective-permute-start.9 = (bf16[128,2304]{1,0:T(8,128)(2,1)S(1)}, bf16[128,2304]{1,0:T(8,128)(2,1)S(1)}, u32[]{:S(2)}, u32[]{:S(2)}) collective-permute-start(bf16[128,2304]{1,0:T(8,128)(2,1)S(1)} %collective-permute-done.5.refs_1_), channel_id=1, source_target_pairs={{0,16},{16,0},{1,17},{17,1},{2,18},{18,2},{3,19},{19,3},{4,20},{20... | collective-permute-start | bytes 1769480 | tf_op jit(solution)/shard_map/ppermute | solution.py:21
  22.4 0.7 collective-permute-start.6
  23.1 0.0 copy-start.1
  23.1 0.0 copy-start.2
  23.2 1.7 %convert_add_fusion = (f32[768,256]{1,0:T(8,128)S(1)}, bf16[768,256]{1,0:T(8,128)(2,1)S(1)}) fusion(f32[768,1024]{1,0:T(8,128)} %copy-done.3, s32[]{:T(128)S(6)} %select_n.92, bf16[768,512]{1,0:T(8,128)(2,1)S(1)} %collective-permute-done, s32[]{:T(128)S(6)} %select_n.93, s32[]{:T(128)S(6)} %select_n.82, s32[]{:T(128)S(6)} %select_n.79), kind=kLoop, calls=%fused_computation.3 | loop fusion | flops 983040 | bytes 3538960 | tf_op jit(solution)/shard_map/add | solution.py:186
  24.9 1.6 %collective-permute-start.4 = (bf16[768,256]{1,0:T(8,128)(2,1)S(1)}, bf16[768,256]{1,0:T(8,128)(2,1)S(1)}, u32[]{:S(2)}, u32[]{:S(2)}) collective-permute-start(bf16[768,256]{1,0:T(8,128)(2,1)S(1)} %get-tuple-element.10.refs_0_), channel_id=1, source_target_pairs={{0,2},{1,3},{2,0},{3,1},{4,6},{5,7},{6,4},{7,5},{8,10},{9,11},{10,... | collective-permute-start | bytes 1179656 | tf_op jit(solution)/shard_map/ppermute | solution.py:21
  26.5 0.5 shard_map.64
  27.7 7.6 %collective-permute-done.2 = bf16[128,2304]{1,0:T(8,128)(2,1)S(1)} collective-permute-done((bf16[128,2304]{1,0:T(8,128)(2,1)}, bf16[128,2304]{1,0:T(8,128)(2,1)S(1)}, u32[]{:S(2)}, u32[]{:S(2)}) %collective-permute-start.2) | collective-permute-done | bytes 589856 | tf_op jit(solution)/shard_map/ppermute | solution.py:162
  35.3 0.1 broadcast_select_fusion.refs_0_
  35.4 1.6 %collective-permute-start.3 = (bf16[128,2304]{1,0:T(8,128)(2,1)S(1)}, bf16[128,2304]{1,0:T(8,128)(2,1)S(1)}, u32[]{:S(2)}, u32[]{:S(2)}) collective-permute-start(bf16[128,2304]{1,0:T(8,128)(2,1)S(1)} %broadcast_select_fusion.refs_0_), channel_id=1, source_target_pairs={{0,16},{16,0},{1,17},{17,1},{2,18},{18,2},{3,19},{19,3},{4,20},{20... | collective-permute-start | bytes 1769480 | tf_op jit(solution)/shard_map/ppermute | solution.py:21
  36.9 0.0 collective-permute-done.6
  37.0 1.3 %collective-permute-start.7 = (bf16[64,2304]{1,0:T(8,128)(2,1)S(1)}, bf16[64,2304]{1,0:T(8,128)(2,1)S(1)}, u32[]{:S(2)}, u32[]{:S(2)}) collective-permute-start(bf16[64,2304]{1,0:T(8,128)(2,1)S(1)} %get-tuple-element.7), channel_id=1, source_target_pairs={{4,0},{8,12},{5,1},{9,13},{6,2},{10,14},{7,3},{11,15},{20,16},{24,... | collective-permute-start | bytes 884744 | tf_op jit(solution)/shard_map/ppermute | solution.py:162
  38.3 1.3 %collective-permute-start.8 = (bf16[64,2304]{1,0:T(8,128)(2,1)S(1)}, bf16[64,2304]{1,0:T(8,128)(2,1)S(1)}, u32[]{:S(2)}, u32[]{:S(2)}) collective-permute-start(bf16[64,2304]{1,0:T(8,128)(2,1)S(1)} %get-tuple-element.8), channel_id=1, source_target_pairs={{4,0},{8,12},{5,1},{9,13},{6,2},{10,14},{7,3},{11,15},{20,16},{24,... | collective-permute-start | bytes 884744 | tf_op jit(solution)/shard_map/ppermute | solution.py:162
  39.6 0.0 collective-permute-done.4.refs_0_.other
  39.6 0.5 shard_map.65
  40.9 3.2 %shard_map.66.refs_4_ = f32[64,768]{1,0:T(8,128)S(1)} custom-call(s32[3]{0:T(128)S(1)} %pad_add_fusion.1.numbers, s32[1,768]{1,0:T(1,128)S(1)} %broadcast_in_dim.44.page, bf16[768,2048]{1,0:T(8,128)(2,1)S(1)} %copy-done.1, bf16[256,2048]{1,0:T(8,128)(2,1)S(1)} %bitcast.27, bf16[128,2304]{1,0:T(8,128)(2,1)S(1)} %collective-permute-done.5.refs_1_, ...), custom_call_target="tpu_custom_call" | custom-call | tf_op jit(solution)/shard_map/pallas_call | solution.py:90
  44.1 5.2 %collective-permute-done.7 = bf16[64,2304]{1,0:T(8,128)(2,1)S(1)} collective-permute-done((bf16[64,2304]{1,0:T(8,128)(2,1)S(1)}, bf16[64,2304]{1,0:T(8,128)(2,1)S(1)}, u32[]{:S(2)}, u32[]{:S(2)}) %collective-permute-start.7) | collective-permute-done | bytes 294944 | tf_op jit(solution)/shard_map/ppermute | solution.py:162
  49.4 0.6 collective-permute-start.10
  49.9 2.7 %collective-permute-done.8 = bf16[64,2304]{1,0:T(8,128)(2,1)S(1)} collective-permute-done((bf16[64,2304]{1,0:T(8,128)(2,1)S(1)}, bf16[64,2304]{1,0:T(8,128)(2,1)S(1)}, u32[]{:S(2)}, u32[]{:S(2)}) %collective-permute-start.8) | collective-permute-done | bytes 294944 | tf_op jit(solution)/shard_map/ppermute | solution.py:162
  52.7 0.6 collective-permute-start.11
  53.3 4.8 %shard_map.67 = f32[64,768]{1,0:T(8,128)S(1)} custom-call(s32[4]{0:T(128)S(1)} %pad_add_fusion.numbers, s32[1,768]{1,0:T(1,128)S(1)} %broadcast_in_dim.44.page, bf16[768,2048]{1,0:T(8,128)(2,1)S(1)} %copy-done.1, bf16[128,2304]{1,0:T(8,128)(2,1)S(1)} %broadcast_select_fusion.refs_0_, bf16[128,2304]{1,0:T(8,128)(2,1)S(1)} %collective-permute-done.3.refs_1_, ...), custom_call_target="tpu_custom_call" | custom-call | tf_op jit(solution)/shard_map/pallas_call | solution.py:90
  58.1 0.7 collective-permute-done.10
  58.8 1.1 %convolution_select_fusion.1 = f32[64,768]{1,0:T(8,128)S(1)} fusion(bf16[768,2048]{1,0:T(8,128)(2,1)S(1)} %copy-done.1, bf16[64,2304]{1,0:T(8,128)(2,1)S(1)} %collective-permute-done.10, pred[768]{0:T(1024)(128)(4,1)S(1)} %get-tuple-element.16), kind=kOutput, calls=%fused_computation.1 | convolution fusion | flops 201375744 | bytes 3605504 | tf_op jit(solution)/shard_map/dot_general | solution.py:226
  59.9 2.1 %collective-permute-done.11 = bf16[64,2304]{1,0:T(8,128)(2,1)S(1)} collective-permute-done((bf16[64,2304]{1,0:T(8,128)(2,1)S(1)}, bf16[64,2304]{1,0:T(8,128)(2,1)S(1)}, u32[]{:S(2)}, u32[]{:S(2)}) %collective-permute-start.11) | collective-permute-done | bytes 294944 | tf_op jit(solution)/shard_map/ppermute | solution.py:21
  62.0 1.1 %add_convert_fusion.1 = bf16[64,768]{1,0:T(8,128)(2,1)S(1)} fusion(f32[64,768]{1,0:T(8,128)S(1)} %shard_map.67, f32[64,768]{1,0:T(8,128)S(1)} %convolution_select_fusion.1, bf16[768,2048]{1,0:T(8,128)(2,1)S(1)} %copy-done.1, bf16[64,2304]{1,0:T(8,128)(2,1)S(1)} %collective-permute-done.11, pred[768]{0:T(1024)(128)(4,1)S(1)} %get-tuple-element.15), kind=kOutput, calls=%fused_computation.14 | convolution fusion | flops 201523200 | bytes 3900416 | tf_op jit(solution)/shard_map/dot_general | solution.py:226
  63.0 1.6 %collective-permute-start.12 = (bf16[64,768]{1,0:T(8,128)(2,1)S(1)}, bf16[64,768]{1,0:T(8,128)(2,1)S(1)}, u32[]{:S(2)}, u32[]{:S(2)}) collective-permute-start(bf16[64,768]{1,0:T(8,128)(2,1)S(1)} %add_convert_fusion.1), channel_id=1, source_target_pairs={{0,2},{1,3},{2,0},{3,1},{4,6},{5,7},{6,4},{7,5},{8,10},{9,11},{10,... | collective-permute-start | bytes 294920 | tf_op jit(solution)/shard_map/ppermute | solution.py:21
  64.6 3.1 %collective-permute-done.12 = bf16[64,768]{1,0:T(8,128)(2,1)S(1)} collective-permute-done((bf16[64,768]{1,0:T(8,128)(2,1)S(1)}, bf16[64,768]{1,0:T(8,128)(2,1)S(1)}, u32[]{:S(2)}, u32[]{:S(2)}) %collective-permute-start.12) | collective-permute-done | bytes 98336 | tf_op jit(solution)/shard_map/ppermute | solution.py:21
  67.7 0.1 collective-permute-start.13
  67.8 1.4 %collective-permute-done.13.other_total = f32[64,768]{1,0:T(8,128)S(1)} collective-permute-done((f32[64,768]{1,0:T(8,128)S(1)}, f32[64,768]{1,0:T(8,128)S(1)}, u32[]{:S(2)}, u32[]{:S(2)}) %collective-permute-start.13) | collective-permute-done | bytes 196640 | tf_op jit(solution)/shard_map/ppermute | solution.py:21
  69.3 1.5 %shard_map.68 = bf16[768,256]{1,0:T(8,128)(2,1)} custom-call(f32[64,768]{1,0:T(8,128)S(1)} %convert_add_fusion.1.total, f32[64,768]{1,0:T(8,128)S(1)} %collective-permute-done.13.other_total, s32[1,768]{1,0:T(1,128)S(1)} %broadcast_in_dim.44.page, f32[1,1024]{1,0:T(1,128)S(1)} %broadcast_in_dim_reshape.3.names, ...), custom_call_target="tpu_custom_call" | custom-call | tf_op jit(solution)/shard_map/pallas_call | solution.py:123
  (31 shorter events, 0.3 us)
Async XLA Ops:
  0.0 1.2 %copy-start = (bf16[4,64,1024]{2,1,0:T(8,128)(2,1)S(1)}, bf16[4,64,1024]{2,1,0:T(8,128)(2,1)}, u32[]{:S(2)}) copy-start(bf16[4,64,1024]{2,1,0:T(8,128)(2,1)} %param.11) | copy-start | bytes 1572868
  1.3 15.7 %collective-permute-start.1 = (bf16[128,2304]{1,0:T(8,128)(2,1)S(1)}, bf16[128,2304]{1,0:T(8,128)(2,1)}, u32[]{:S(2)}, u32[]{:S(2)}) collective-permute-start(bf16[128,2304]{1,0:T(8,128)(2,1)S(1)} %pad_maximum_fusion.1), channel_id=1, source_target_pairs={{4,8},{8,4},{5,9},{9,5},{6,10},{10,6},{7,11},{11,7},{20,24},{24,20... | collective-permute-start | bytes 1769480 | tf_op jit(solution)/shard_map/ppermute | solution.py:165
  2.7 18.1 %collective-permute-start.5 = (bf16[128,2304]{1,0:T(8,128)(2,1)S(1)}, bf16[128,2304]{1,0:T(8,128)(2,1)S(1)}, u32[]{:S(2)}, u32[]{:S(2)}) collective-permute-start(bf16[128,2304]{1,0:T(8,128)(2,1)S(1)} %pad_maximum_fusion.1), channel_id=1, source_target_pairs={{0,4},{4,0},{8,12},{12,8},{1,5},{5,1},{9,13},{13,9},{2,6},{6,2},{1... | collective-permute-start | bytes 1769480 | tf_op jit(solution)/shard_map/ppermute | solution.py:21
  14.0 1.6 %copy-start.3 = (f32[768,1024]{1,0:T(8,128)}, f32[768,1024]{1,0:T(8,128)S(1)}, u32[]{:S(2)}) copy-start(f32[768,1024]{1,0:T(8,128)S(1)} %fusion.5) | copy-start | bytes 9437188
  15.6 0.7 copy-start.4
  15.6 0.7 copy-start.5
  15.8 7.3 %collective-permute-start = (bf16[768,512]{1,0:T(8,128)(2,1)S(1)}, bf16[768,512]{1,0:T(8,128)(2,1)S(1)}, u32[]{:S(2)}, u32[]{:S(2)}) collective-permute-start(bf16[768,512]{1,0:T(8,128)(2,1)S(1)} %pad_maximum_fusion), channel_id=1, source_target_pairs={{0,1},{1,0},{2,3},{3,2},{4,5},{5,4},{6,7},{7,6},{8,9},{9,8},{10,11... | collective-permute-start | bytes 2359304 | tf_op jit(solution)/shard_map/ppermute | solution.py:21
  16.9 18.3 %collective-permute-start.2 = (bf16[128,2304]{1,0:T(8,128)(2,1)}, bf16[128,2304]{1,0:T(8,128)(2,1)S(1)}, u32[]{:S(2)}, u32[]{:S(2)}) collective-permute-start(bf16[128,2304]{1,0:T(8,128)(2,1)} %collective-permute-done.1), channel_id=1, source_target_pairs={{4,0},{8,12},{5,1},{9,13},{6,2},{10,14},{7,3},{11,15},{20,16},{24,... | collective-permute-start | bytes 1769480 | tf_op jit(solution)/shard_map/ppermute | solution.py:162
  20.9 18.7 %collective-permute-start.9 = (bf16[128,2304]{1,0:T(8,128)(2,1)S(1)}, bf16[128,2304]{1,0:T(8,128)(2,1)S(1)}, u32[]{:S(2)}, u32[]{:S(2)}) collective-permute-start(bf16[128,2304]{1,0:T(8,128)(2,1)S(1)} %collective-permute-done.5.refs_1_), channel_id=1, source_target_pairs={{0,16},{16,0},{1,17},{17,1},{2,18},{18,2},{3,19},{19,3},{4,20},{20... | collective-permute-start | bytes 1769480 | tf_op jit(solution)/shard_map/ppermute | solution.py:21
  22.4 14.5 %collective-permute-start.6 = (bf16[128,2304]{1,0:T(8,128)(2,1)S(1)}, bf16[128,2304]{1,0:T(8,128)(2,1)S(1)}, u32[]{:S(2)}, u32[]{:S(2)}) collective-permute-start(bf16[128,2304]{1,0:T(8,128)(2,1)S(1)} %collective-permute-done.5.refs_1_), channel_id=1, source_target_pairs={{4,8},{8,4},{5,9},{9,5},{6,10},{10,6},{7,11},{11,7},{20,24},{24,20... | collective-permute-start | bytes 1769480 | tf_op jit(solution)/shard_map/ppermute | solution.py:165
  23.1 17.7 %copy-start.1 = (bf16[768,2048]{1,0:T(8,128)(2,1)S(1)}, bf16[768,2048]{1,0:T(8,128)(2,1)}, u32[]{:S(2)}) copy-start(bf16[768,2048]{1,0:T(8,128)(2,1)} %tokens.3) | copy-start | bytes 9437188
  23.1 17.7 %copy-start.2 = (bf16[4,64,2048]{2,1,0:T(8,128)(2,1)S(1)}, bf16[4,64,2048]{2,1,0:T(8,128)(2,1)}, u32[]{:S(2)}) copy-start(bf16[4,64,2048]{2,1,0:T(8,128)(2,1)} %param.10) | copy-start | bytes 3145732
  24.9 14.7 %collective-permute-start.4 = (bf16[768,256]{1,0:T(8,128)(2,1)S(1)}, bf16[768,256]{1,0:T(8,128)(2,1)S(1)}, u32[]{:S(2)}, u32[]{:S(2)}) collective-permute-start(bf16[768,256]{1,0:T(8,128)(2,1)S(1)} %get-tuple-element.10.refs_0_), channel_id=1, source_target_pairs={{0,2},{1,3},{2,0},{3,1},{4,6},{5,7},{6,4},{7,5},{8,10},{9,11},{10,... | collective-permute-start | bytes 1179656 | tf_op jit(solution)/shard_map/ppermute | solution.py:21
  35.4 17.9 %collective-permute-start.3 = (bf16[128,2304]{1,0:T(8,128)(2,1)S(1)}, bf16[128,2304]{1,0:T(8,128)(2,1)S(1)}, u32[]{:S(2)}, u32[]{:S(2)}) collective-permute-start(bf16[128,2304]{1,0:T(8,128)(2,1)S(1)} %broadcast_select_fusion.refs_0_), channel_id=1, source_target_pairs={{0,16},{16,0},{1,17},{17,1},{2,18},{18,2},{3,19},{19,3},{4,20},{20... | collective-permute-start | bytes 1769480 | tf_op jit(solution)/shard_map/ppermute | solution.py:21
  37.0 12.3 %collective-permute-start.7 = (bf16[64,2304]{1,0:T(8,128)(2,1)S(1)}, bf16[64,2304]{1,0:T(8,128)(2,1)S(1)}, u32[]{:S(2)}, u32[]{:S(2)}) collective-permute-start(bf16[64,2304]{1,0:T(8,128)(2,1)S(1)} %get-tuple-element.7), channel_id=1, source_target_pairs={{4,0},{8,12},{5,1},{9,13},{6,2},{10,14},{7,3},{11,15},{20,16},{24,... | collective-permute-start | bytes 884744 | tf_op jit(solution)/shard_map/ppermute | solution.py:162
  38.3 14.4 %collective-permute-start.8 = (bf16[64,2304]{1,0:T(8,128)(2,1)S(1)}, bf16[64,2304]{1,0:T(8,128)(2,1)S(1)}, u32[]{:S(2)}, u32[]{:S(2)}) collective-permute-start(bf16[64,2304]{1,0:T(8,128)(2,1)S(1)} %get-tuple-element.8), channel_id=1, source_target_pairs={{4,0},{8,12},{5,1},{9,13},{6,2},{10,14},{7,3},{11,15},{20,16},{24,... | collective-permute-start | bytes 884744 | tf_op jit(solution)/shard_map/ppermute | solution.py:162
  49.4 9.4 %collective-permute-start.10 = (bf16[64,2304]{1,0:T(8,128)(2,1)S(1)}, bf16[64,2304]{1,0:T(8,128)(2,1)S(1)}, u32[]{:S(2)}, u32[]{:S(2)}) collective-permute-start(bf16[64,2304]{1,0:T(8,128)(2,1)S(1)} %broadcast_select_fusion.2.refs_2_), channel_id=1, source_target_pairs={{0,16},{16,0},{1,17},{17,1},{2,18},{18,2},{3,19},{19,3},{4,20},{20... | collective-permute-start | bytes 884744 | tf_op jit(solution)/shard_map/ppermute | solution.py:21
  52.7 9.3 %collective-permute-start.11 = (bf16[64,2304]{1,0:T(8,128)(2,1)S(1)}, bf16[64,2304]{1,0:T(8,128)(2,1)S(1)}, u32[]{:S(2)}, u32[]{:S(2)}) collective-permute-start(bf16[64,2304]{1,0:T(8,128)(2,1)S(1)} %broadcast_select_fusion.1.refs_3_), channel_id=1, source_target_pairs={{0,16},{16,0},{1,17},{17,1},{2,18},{18,2},{3,19},{19,3},{4,20},{20... | collective-permute-start | bytes 884744 | tf_op jit(solution)/shard_map/ppermute | solution.py:21
  63.0 4.7 %collective-permute-start.12 = (bf16[64,768]{1,0:T(8,128)(2,1)S(1)}, bf16[64,768]{1,0:T(8,128)(2,1)S(1)}, u32[]{:S(2)}, u32[]{:S(2)}) collective-permute-start(bf16[64,768]{1,0:T(8,128)(2,1)S(1)} %add_convert_fusion.1), channel_id=1, source_target_pairs={{0,2},{1,3},{2,0},{3,1},{4,6},{5,7},{6,4},{7,5},{8,10},{9,11},{10,... | collective-permute-start | bytes 294920 | tf_op jit(solution)/shard_map/ppermute | solution.py:21
  67.7 1.5 %collective-permute-start.13 = (f32[64,768]{1,0:T(8,128)S(1)}, f32[64,768]{1,0:T(8,128)S(1)}, u32[]{:S(2)}, u32[]{:S(2)}) collective-permute-start(f32[64,768]{1,0:T(8,128)S(1)} %convert_add_fusion.1.total), channel_id=1, source_target_pairs={{0,1},{1,0},{2,3},{3,2},{4,5},{5,4},{6,7},{7,6},{8,9},{9,8},{10,11... | collective-permute-start | bytes 589832 | tf_op jit(solution)/shard_map/ppermute | solution.py:21
